TPU v7x, 256 devices: a whole 4x4x8 slice. The times are simulated.
256 devices in a mesh: section: 4 (over z_lo, core), dp: 64 (over x, y, z_hi).
Axes of the slice: x: 4, y: 4, z: 8 (z_hi: 4, z_lo: 2; z = z_hi * 2 + z_lo), core: 2. Of those that a mesh axis runs over, the one named last changes fastest.
Arguments:
- images: bfloat16 [2, 64, 12, 3840], P(None, 'dp'), may hold values from -6 to 6
- targets: bfloat16 [2, 64, 12, 3840], P(None, 'dp'), may hold values from -6 to 6
- kernels: bfloat16 [4, 2880, 640], P('section'), may hold values from -0.109375 to 0.109375
Outputs:
- kernel_grad: float32 [4, 2880, 640], P('section', 'dp')
All inputs are finite; a program needn't handle non-finite values.
Results may differ from a plain program's by a relative error of at most 0.0075.
Values may be sent and summed in bfloat16 or wider, within the bound.
A program may use at most 128 MiB of HBM per device.

v0:
```python
import jax
import jax.numpy as jnp
import numpy as np
from jax import lax
from jax.experimental import pallas as pl
from jax.experimental.pallas import tpu as pltpu
from jax.sharding import PartitionSpec as P

MESH = pl.DeviceIdType.MESH
ROWS = 80
CH = 320
GW = 384
TAPS = 9
SHARE = 45
SLOT = 48


def phase_shift(phase, tap):
    alpha, beta = divmod(phase, 2)
    a, b = divmod(tap, 3)
    return ((alpha + a - 1) // 2 + 1) * 3 + ((beta + b - 1) // 2 + 1)


def tables():
    shift = np.zeros((TAPS, ROWS, ROWS), np.float32)
    encode = np.zeros((TAPS, ROWS, 288), np.float32)
    order = np.zeros((4, ROWS, 288), np.float32)
    for n in range(2):
        for i in range(6):
            for j in range(6):
                r = n * 36 + i * 6 + j
                for tap in range(TAPS):
                    a, b = divmod(tap, 3)
                    ii, jj = i + a - 1, j + b - 1
                    if 0 <= ii < 6 and 0 <= jj < 6:
                        shift[tap, r, n * 36 + ii * 6 + jj] = 1
                    ii, jj = 2 * i + a - 1, 2 * j + b - 1
                    if 0 <= ii < 12 and 0 <= jj < 12:
                        encode[tap, r, n * 144 + ii * 12 + jj] = 1
                for phase in range(4):
                    alpha, beta = divmod(phase, 2)
                    order[phase, r, n * 144 + (2 * i + alpha) * 12 + 2 * j + beta] = 1
    fold = np.zeros((TAPS, ROWS, 4, ROWS), np.float32)
    for tap in range(TAPS):
        for phase in range(4):
            fold[tap, :, phase, :] = shift[phase_shift(phase, tap)].T
    return (
        shift.reshape(TAPS * ROWS, ROWS),
        encode.reshape(TAPS * ROWS, 288),
        fold.reshape(TAPS * ROWS, 4 * ROWS),
        order.reshape(4 * ROWS, 288),
    )


def silu(v):
    return v * jax.nn.sigmoid(v)


def silu_slope(v):
    g = jax.nn.sigmoid(v)
    return g * (1.0 + v * (1.0 - g))


def mm(a, b):
    return jnp.dot(a, b, preferred_element_type=jnp.float32)


def mm_nt(a, b):
    return lax.dot_general(a, b, (((1,), (1,)), ((), ())), preferred_element_type=jnp.float32)


def mm_tn(a, b):
    return lax.dot_general(a, b, (((0,), (0,)), ((), ())), preferred_element_type=jnp.float32)


def remote(src, dst, send_sem, recv_sem, device):
    return pltpu.make_async_remote_copy(
        src_ref=src, dst_ref=dst, send_sem=send_sem, recv_sem=recv_sem, device_id=device, device_id_type=MESH
    )


def body(
    img, tgt, ker, c_shift, c_encode, c_fold, c_order, out,
    w_in, x_in, t_in, s_shift, s_encode, s_fold, s_order,
    wp, feat, act, pre, delta3, zed, target,
    h_in, skip_in, g_in, gskip_in, h_out, g_out,
    gx, gh, gd, gz, left, grad, pack, y_buf, y_sum, z_out, z_buf,
    load_sem, hop_send, hop_recv, a_send, a_recv, d_send, d_recv, y_send, y_recv, z_send, z_recv,
):
    bf = jnp.bfloat16
    f32 = jnp.float32
    sec = lax.axis_index("section")
    dp = lax.axis_index("dp")
    x, y, z = dp // 16, (dp // 4) % 4, dp % 4

    def x_peer(k):
        p = (x + k) % 4
        return p, {"dp": p * 16 + y * 4 + z}

    def y_peer(k):
        p = (y + k) % 4
        return p, {"dp": x * 16 + p * 4 + z}

    def z_peer(k):
        p = (z + k) % 4
        return p, {"dp": x * 16 + y * 4 + p}

    def load(src, dst, n):
        return pltpu.make_async_copy(src, dst, load_sem.at[n])

    w_load = load(ker, w_in, 0)
    w_load.start()

    barrier = pltpu.get_barrier_semaphore()
    for k in range(1, 4):
        pl.semaphore_signal(barrier, inc=1, device_id={"section": (sec + k) % 4}, device_id_type=MESH)
        for peer in (x_peer, y_peer, z_peer):
            pl.semaphore_signal(barrier, inc=1, device_id=peer(k)[1], device_id_type=MESH)
    pl.semaphore_wait(barrier, 12)

    row0 = pl.multiple_of(x * 160, 16)

    def gather_start(src, buf, send, recv):
        copies = []
        for k in range(1, 4):
            p, dev = x_peer(k)
            copy = remote(src, buf.at[x], send.at[p], recv.at[x], dev)
            copy.start()
            copies.append(copy)
        return copies

    def gather_wait(k, src, buf, send, recv):
        p, dev = x_peer(k)
        remote(src, buf.at[p], send.at[p], recv.at[p], dev).wait_recv()
        return p

    def group(g):
        return slice(g * GW, (g + 1) * GW)

    def pack_weights():
        lane = lax.broadcasted_iota(jnp.int32, (CH, GW), 1)

        def one(t, carry):
            rows = pl.ds(pl.multiple_of(t * CH, 16), CH)
            base = pl.multiple_of(t * GW, 16)
            first = w_in[rows, 0:GW].astype(f32)
            wp[0, pl.ds(base, CH), :] = jnp.where(lane < CH, first, 0.0).astype(bf)
            second = pltpu.roll(w_in[rows, 256:640].astype(f32), GW - 64, 1)
            wp[1, pl.ds(base, CH), :] = jnp.where(lane < CH, second, 0.0).astype(bf)
            for g in range(2):
                wp[g, pl.ds(base + CH, GW - CH), :] = jnp.zeros((GW - CH, GW), bf)
            return carry

        lax.fori_loop(0, TAPS, one, 0)

    def left_shift(p):
        part = mm(s_shift[pl.ds(row0, 240), :], gh[p]).astype(bf)
        for k in range(3):
            left[k, pl.ds(pl.multiple_of(p * ROWS, 16), ROWS), :] = part[k * ROWS:(k + 1) * ROWS]

    def left_encode(p):
        part = mm(s_encode[pl.ds(row0, 240), :], gx[p]).astype(bf)
        for k in range(3):
            left[k, pl.ds(pl.multiple_of(p * ROWS, 16), ROWS), 0:GW] = part[k * ROWS:(k + 1) * ROWS]

    @pl.when(sec == 0)
    def encoder():
        loads = [load(img, x_in, 1), load(c_encode, s_encode, 2)]
        for copy in loads:
            copy.start()
        for copy in loads:
            copy.wait()
        e_all = mm(s_encode[...], x_in[...]).astype(bf)
        w_load.wait()
        acc = jnp.zeros((ROWS, 2 * CH), f32)
        for t in range(TAPS):
            acc = acc + mm(e_all[t * ROWS:(t + 1) * ROWS, 0:CH], w_in[t * CH:(t + 1) * CH, :])
        wide = jnp.concatenate([acc, jnp.zeros((ROWS, 128), f32)], axis=1)
        moved = pltpu.roll(wide, 64, 1)
        lane = lax.broadcasted_iota(jnp.int32, (ROWS, 2 * GW), 1)
        wide = jnp.where(lane < CH, wide, jnp.where((lane >= GW) & (lane < GW + CH), moved, 0.0))
        act[...] = wide
        h_out[...] = silu(wide).astype(bf)
        sends = [
            remote(h_out, h_in, hop_send.at[0], hop_recv.at[0], {"section": 1}),
            remote(h_out, skip_in, hop_send.at[1], hop_recv.at[1], {"section": 3}),
        ]
        for copy in sends:
            copy.start()
        sends += gather_start(x_in, gx, a_send, a_recv)
        gx[x] = x_in[...]
        left_encode(x)
        for k in range(1, 4):
            left_encode(gather_wait(k, x_in, gx, a_send, a_recv))
        remote(g_out, gskip_in, hop_send.at[3], hop_recv.at[3], {"section": 3}).wait_recv()
        remote(g_out, g_in, hop_send.at[2], hop_recv.at[2], {"section": 1}).wait_recv()
        total = g_in[...].astype(f32) + gskip_in[...].astype(f32)
        h_in[...] = (total * silu_slope(act[...])).astype(bf)
        sends += gather_start(h_in, gd, d_send, d_recv)
        gd[x] = h_in[...]
        for k in range(1, 4):
            gather_wait(k, h_in, gd, d_send, d_recv)
        right = gd[...].reshape(4 * ROWS, 2 * GW)
        for k in range(3):
            grad[k * CH:(k + 1) * CH, :] = mm_tn(left[k, :, 0:GW], right)[0:CH]
        for copy in sends:
            copy.wait_send()

    @pl.when((sec == 1) | (sec == 2))
    def centre():
        s_load = load(c_shift, s_shift, 1)
        s_load.start()
        w_load.wait()
        pack_weights()
        s_load.wait()
        remote(h_out, h_in, hop_send.at[0], hop_recv.at[0], {"section": sec - 1}).wait_recv()
        h = h_in[...]
        shifted = mm(s_shift[...], h).astype(bf)
        for g in range(2):
            for t in range(TAPS):
                feat[g, 0:ROWS, t * GW:(t + 1) * GW] = shifted[t * ROWS:(t + 1) * ROWS, group(g)]
            pre_g = mm(feat[g, 0:ROWS, :], wp[g])
            act[:, group(g)] = pre_g
            h_out[:, group(g)] = (h[:, group(g)].astype(f32) + silu(pre_g)).astype(bf)
        hop = remote(h_out, h_in, hop_send.at[0], hop_recv.at[0], {"section": sec + 1})
        hop.start()
        sends = [hop]
        sends += gather_start(h_in, gh, a_send, a_recv)
        gh[x] = h
        left_shift(x)
        for k in range(1, 4):
            left_shift(gather_wait(k, h_in, gh, a_send, a_recv))
        remote(g_out, g_in, hop_send.at[2], hop_recv.at[2], {"section": sec + 1}).wait_recv()
        delta = (g_in[...].astype(f32) * silu_slope(act[...])).astype(bf)
        skip_in[...] = delta
        sends += gather_start(skip_in, gd, d_send, d_recv)
        back = mm(s_shift[...], delta).astype(bf)
        for g in range(2):
            acc = g_in[:, group(g)].astype(f32)
            for t in range(TAPS):
                piece = back[(8 - t) * ROWS:(9 - t) * ROWS, group(g)]
                acc = acc + mm_nt(piece, wp[g, t * GW:(t + 1) * GW, :])
            g_out[:, group(g)] = acc.astype(bf)
        hop = remote(g_out, g_in, hop_send.at[2], hop_recv.at[2], {"section": sec - 1})
        hop.start()
        sends.append(hop)
        gd[x] = delta
        for k in range(1, 4):
            gather_wait(k, skip_in, gd, d_send, d_recv)
        for g in range(2):
            right = gd[:, :, group(g)].reshape(4 * ROWS, GW)
            for k in range(3):
                grad[k * CH:(k + 1) * CH, group(g)] = mm_tn(left[k, :, group(g)], right)[0:CH]
        for copy in sends:
            copy.wait_send()

    @pl.when(sec == 3)
    def decoder():
        loads = [load(c_shift, s_shift, 1), load(c_fold, s_fold, 2), load(c_order, s_order, 3), load(tgt, t_in, 4)]
        for copy in loads:
            copy.start()
        w_load.wait()
        pack_weights()
        for copy in loads:
            copy.wait()
        target[...] = mm(s_order[...], t_in[...])
        remote(h_out, skip_in, hop_send.at[1], hop_recv.at[1], {"section": 0}).wait_recv()
        remote(h_out, h_in, hop_send.at[0], hop_recv.at[0], {"section": 2}).wait_recv()
        u = (h_in[...].astype(f32) + skip_in[...].astype(f32)).astype(bf)
        h_out[...] = u
        sends = gather_start(h_out, gh, a_send, a_recv)
        gh[x] = u
        shifted = mm(s_shift[...], u).astype(bf)
        for g in range(2):
            for phase in range(4):
                for t in range(TAPS):
                    s = phase_shift(phase, t)
                    feat[g, phase * ROWS:(phase + 1) * ROWS, t * GW:(t + 1) * GW] = shifted[
                        s * ROWS:(s + 1) * ROWS, group(g)
                    ]
            pre[g] = mm(feat[g], wp[g])
        value, gate = pre[0], pre[1]
        sig = jax.nn.sigmoid(gate)
        act_gate = gate * sig
        residual = (value * act_gate - target[...]) * (1.0 / 128.0)
        delta3[:, 0:GW] = (residual * act_gate).astype(bf)
        delta3[:, GW:] = (residual * value * (sig * (1.0 + gate * (1.0 - sig)))).astype(bf)
        zed[...] = mm(s_fold[...], delta3[...]).astype(bf)
        for k in range(1, 4):
            p, dev = x_peer(k)
            rows = pl.ds(pl.multiple_of(p * 160, 16), 240)
            copy = remote(zed.at[rows], gz.at[x], d_send.at[p], d_recv.at[x], dev)
            copy.start()
            sends.append(copy)
        for g in range(2):
            acc = jnp.zeros((ROWS, GW), f32)
            for t in range(TAPS):
                acc = acc + mm_nt(zed[t * ROWS:(t + 1) * ROWS, group(g)], wp[g, t * GW:(t + 1) * GW, :])
            g_out[:, group(g)] = acc.astype(bf)
        hops = [
            remote(g_out, g_in, hop_send.at[2], hop_recv.at[2], {"section": 2}),
            remote(g_out, gskip_in, hop_send.at[3], hop_recv.at[3], {"section": 0}),
        ]
        for copy in hops:
            copy.start()
        sends += hops
        gz[x] = zed[pl.ds(row0, 240), :]
        for k in range(1, 4):
            gather_wait(k, h_out, gh, a_send, a_recv)
            p, dev = x_peer(k)
            remote(zed.at[0:240], gz.at[p], d_send.at[p], d_recv.at[p], dev).wait_recv()
        for g in range(2):
            lhs = gh[:, :, group(g)].reshape(4 * ROWS, GW)
            for k in range(3):
                right = gz[:, k * ROWS:(k + 1) * ROWS, group(g)].reshape(4 * ROWS, GW)
                grad[k * CH:(k + 1) * CH, group(g)] = mm_tn(lhs, right)[0:CH]
        for copy in sends:
            copy.wait_send()

    grad[960:976, :] = jnp.zeros((16, 2 * GW), f32)
    lane = lax.broadcasted_iota(jnp.int32, (SLOT, 2 * GW), 1)
    for k in range(16):
        odd = (SHARE * k) % 8
        rows = pl.ds(pl.multiple_of(x * 80 + (SHARE * k - odd), 8), 56)
        part = grad[rows, :]
        if odd:
            part = pltpu.roll(part, 56 - odd, 0)
        part = part[0:SLOT]
        moved = pltpu.roll(part, 2 * GW - 64, 1)
        pack[k] = jnp.where(lane < CH, part, moved)[:, 0:2 * CH].astype(bf)

    sends = []
    for k in range(1, 4):
        p, dev = y_peer(k)
        copy = remote(pack.at[pl.ds(p * 4, 4)], y_buf.at[y], y_send.at[p], y_recv.at[y], dev)
        copy.start()
        sends.append(copy)
    y_sum[...] = pack[pl.ds(y * 4, 4)].astype(f32)
    for k in range(1, 4):
        p, dev = y_peer(k)
        remote(pack.at[pl.ds(0, 4)], y_buf.at[p], y_send.at[p], y_recv.at[p], dev).wait_recv()
        y_sum[...] += y_buf[p].astype(f32)
    z_out[...] = y_sum[...].astype(bf)
    for k in range(1, 4):
        p, dev = z_peer(k)
        copy = remote(z_out.at[p], z_buf.at[z], z_send.at[p], z_recv.at[z], dev)
        copy.start()
        sends.append(copy)
    total = y_sum[z]
    for k in range(1, 4):
        p, dev = z_peer(k)
        remote(z_out.at[p], z_buf.at[p], z_send.at[p], z_recv.at[p], dev).wait_recv()
        total = total + z_buf[p].astype(f32)
    out[...] = total[0:SHARE]
    for copy in sends:
        copy.wait_send()


def on_device(images, targets, kernels):
    bf = jnp.bfloat16

    def cells(grids):
        return jnp.pad(grids.reshape(288, CH), ((0, 0), (0, GW - CH)))

    consts = [jnp.asarray(t, bf) for t in tables()]
    vm = pltpu.VMEM
    dma = pltpu.SemaphoreType.DMA
    hop = vm((ROWS, 2 * GW), bf)
    result = pl.pallas_call(
        body,
        out_shape=jax.ShapeDtypeStruct((SHARE, 2 * CH), jnp.float32),
        in_specs=[pl.BlockSpec(memory_space=pl.ANY)] * 7,
        out_specs=pl.BlockSpec(memory_space=pltpu.VMEM),
        scratch_shapes=[
            vm((TAPS * CH, 2 * CH), bf),
            vm((288, GW), bf),
            vm((288, GW), bf),
            vm((TAPS * ROWS, ROWS), bf),
            vm((TAPS * ROWS, 288), bf),
            vm((TAPS * ROWS, 4 * ROWS), bf),
            vm((4 * ROWS, 288), bf),
            vm((2, TAPS * GW, GW), bf),
            vm((2, 4 * ROWS, TAPS * GW), bf),
            vm((ROWS, 2 * GW), jnp.float32),
            vm((2, 4 * ROWS, GW), jnp.float32),
            vm((4 * ROWS, 2 * GW), bf),
            vm((TAPS * ROWS, 2 * GW), bf),
            vm((4 * ROWS, GW), jnp.float32),
            hop, hop, hop, hop, hop, hop,
            vm((4, 288, GW), bf),
            vm((4, ROWS, 2 * GW), bf),
            vm((4, ROWS, 2 * GW), bf),
            vm((4, 240, 2 * GW), bf),
            vm((3, 4 * ROWS, 2 * GW), bf),
            vm((976, 2 * GW), jnp.float32),
            vm((16, SLOT, 2 * CH), bf),
            vm((4, 4, SLOT, 2 * CH), bf),
            vm((4, SLOT, 2 * CH), jnp.float32),
            vm((4, SLOT, 2 * CH), bf),
            vm((4, SLOT, 2 * CH), bf),
            dma((8,)), dma((4,)), dma((4,)),
            dma((4,)), dma((4,)), dma((4,)), dma((4,)), dma((4,)), dma((4,)), dma((4,)), dma((4,)),
        ],
        compiler_params=pltpu.CompilerParams(
            collective_id=0, has_side_effects=True, vmem_limit_bytes=48 * 1024 * 1024
        ),
    )(cells(images), cells(targets), kernels[0], *consts)
    return result[None]


def solution(mesh):
    return jax.shard_map(
        on_device,
        mesh=mesh,
        in_specs=(P(None, "dp", None, None), P(None, "dp", None, None), P("section", None, None)),
        out_specs=P("section", "dp", None),
        check_vma=False,
    )
```

profile of v0, /device:TPU:8, one launch (start us, length us, event | category | flops | bytes accessed | tf_op | source)
XLA Modules:
  0.0 68.6 jit_solution(1875026057468327833)
XLA Ops:
  0.0 0.9 %copy.11 = bf16[2,1,12,3840]{3,2,0,1:T(8,128)(2,1)S(1)} copy(bf16[2,1,12,3840]{3,0,2,1:T(2,128)(2,1)} %param.7) | data formatting | bytes 368640 | tf_op args[0]
  1.0 0.3 reshape.6
  1.3 1.0 %copy.12 = bf16[2,1,12,3840]{3,2,0,1:T(8,128)(2,1)S(1)} copy(bf16[2,1,12,3840]{3,0,2,1:T(2,128)(2,1)} %param.8) | data formatting | bytes 368640 | tf_op args[1]
  2.3 0.3 reshape.7
  2.6 0.0 copy-start
  2.6 2.0 %copy-done = bf16[1,2880,640]{2,1,0:T(8,128)(2,1)S(1)} copy-done((bf16[1,2880,640]{2,1,0:T(8,128)(2,1)S(1)}, bf16[1,2880,640]{2,1,0:T(8,128)(2,1)}, u32[]{:S(2)}) %copy-start) | copy-done | bytes 3686424
  4.6 0.0 copy-start.1
  4.6 1.0 %copy-done.1 = bf16[720,320]{1,0:T(8,128)(2,1)S(1)} copy-done((bf16[720,320]{1,0:T(8,128)(2,1)S(1)}, bf16[720,320]{1,0:T(8,128)(2,1)}, u32[]{:S(2)}) %copy-start.1) | copy-done | bytes 460824
  5.7 0.0 copy-start.2
  5.7 1.0 %copy-done.2 = bf16[720,288]{1,0:T(8,128)(2,1)S(1)} copy-done((bf16[720,288]{1,0:T(8,128)(2,1)S(1)}, bf16[720,288]{1,0:T(8,128)(2,1)}, u32[]{:S(2)}) %copy-start.2) | copy-done | bytes 414744
  6.8 0.0 copy-start.3
  6.8 0.9 %copy-done.3 = bf16[320,288]{1,0:T(8,128)(2,1)S(1)} copy-done((bf16[320,288]{1,0:T(8,128)(2,1)S(1)}, bf16[320,288]{1,0:T(8,128)(2,1)}, u32[]{:S(2)}) %copy-start.3) | copy-done | bytes 184344
  7.7 0.0 copy-start.4
  7.7 0.9 %copy-done.4 = bf16[720,80]{1,0:T(8,128)(2,1)S(1)} copy-done((bf16[720,80]{1,0:T(8,128)(2,1)S(1)}, bf16[720,80]{1,0:T(8,128)(2,1)}, u32[]{:S(2)}) %copy-start.4) | copy-done | bytes 115224
  8.6 59.2 %shard_map.73 = f32[45,640]{1,0:T(8,128)S(1)} custom-call(bf16[288,384]{1,0:T(8,128)(2,1)S(1)} %pad.7.img, bf16[288,384]{1,0:T(8,128)(2,1)S(1)} %pad.8.tgt, bf16[2880,640]{1,0:T(8,128)(2,1)S(1)} %bitcast.6, bf16[720,80]{1,0:T(8,128)(2,1)S(1)} %copy-done.4, bf16[720,288]{1,0:T(8,128)(2,1)S(1)} %copy-done.2, bf16[720,320]{1,0:T(8,128)(2,1)S(1)} %copy-done.1, ...), custom_call_target="tpu_custom_call" | custom-call | tf_op jit(solution)/shard_map/pallas_call | solution.py:369
  67.8 0.8 %copy.13 = f32[1,45,640]{2,0,1:T(1,128)} copy(f32[1,45,640]{2,1,0:T(8,128)S(1)} %bitcast.7) | data formatting | bytes 230400 | tf_op jit(solution)/shard_map/broadcast_in_dim | solution.py:408
  (2 shorter events, 0.1 us)
Async XLA Ops:
  2.6 2.0 %copy-start = (bf16[1,2880,640]{2,1,0:T(8,128)(2,1)S(1)}, bf16[1,2880,640]{2,1,0:T(8,128)(2,1)}, u32[]{:S(2)}) copy-start(bf16[1,2880,640]{2,1,0:T(8,128)(2,1)} %param.9) | copy-start | bytes 11059204
  4.6 1.1 %copy-start.1 = (bf16[720,320]{1,0:T(8,128)(2,1)S(1)}, bf16[720,320]{1,0:T(8,128)(2,1)}, u32[]{:S(2)}) copy-start(bf16[720,320]{1,0:T(8,128)(2,1)} %constant.13.clone.c_fold) | copy-start | bytes 1382404
  5.7 1.1 %copy-start.2 = (bf16[720,288]{1,0:T(8,128)(2,1)S(1)}, bf16[720,288]{1,0:T(8,128)(2,1)}, u32[]{:S(2)}) copy-start(bf16[720,288]{1,0:T(8,128)(2,1)} %constant.12.clone.c_encode) | copy-start | bytes 1244164
  6.8 0.9 %copy-start.3 = (bf16[320,288]{1,0:T(8,128)(2,1)S(1)}, bf16[320,288]{1,0:T(8,128)(2,1)}, u32[]{:S(2)}) copy-start(bf16[320,288]{1,0:T(8,128)(2,1)} %constant.14.clone.c_order) | copy-start | bytes 552964
  7.7 0.9 %copy-start.4 = (bf16[720,80]{1,0:T(8,128)(2,1)S(1)}, bf16[720,80]{1,0:T(8,128)(2,1)}, u32[]{:S(2)}) copy-start(bf16[720,80]{1,0:T(8,128)(2,1)} %constant.11.clone.c_shift) | copy-start | bytes 345604
where the time goes:
time: 68.9 us; the launch traced here: 68.6 us
  Pallas kernels  59.2 us (86%)
  local copies, waits for them, and re-layouts  9.35 us (14%)
    pallas_call x1, Pallas kernels, on_device(): pl.pallas_call(body, out_shape=jax.ShapeDtypeStruct((SHARE, 2 * CH), jnp....  59.2 us
    unnamed x12, local copies, waits for them, and re-layouts  7.91 us

commit v1 on v0

--- a/solution.py
+++ b/solution.py
@@ -13,6 +13,7 @@
 TAPS = 9
 SHARE = 45
 SLOT = 48
+CELLS = 12 * 32
 
 
 def phase_shift(phase, tap):
@@ -23,8 +24,8 @@
 
 def tables():
     shift = np.zeros((TAPS, ROWS, ROWS), np.float32)
-    encode = np.zeros((TAPS, ROWS, 288), np.float32)
-    order = np.zeros((4, ROWS, 288), np.float32)
+    encode = np.zeros((TAPS, ROWS, CELLS), np.float32)
+    order = np.zeros((4, ROWS, CELLS), np.float32)
     for n in range(2):
         for i in range(6):
             for j in range(6):
@@ -36,19 +37,19 @@
                         shift[tap, r, n * 36 + ii * 6 + jj] = 1
                     ii, jj = 2 * i + a - 1, 2 * j + b - 1
                     if 0 <= ii < 12 and 0 <= jj < 12:
-                        encode[tap, r, n * 144 + ii * 12 + jj] = 1
+                        encode[tap, r, jj * 32 + n * 16 + ii] = 1
                 for phase in range(4):
                     alpha, beta = divmod(phase, 2)
-                    order[phase, r, n * 144 + (2 * i + alpha) * 12 + 2 * j + beta] = 1
+                    order[phase, r, (2 * j + beta) * 32 + n * 16 + 2 * i + alpha] = 1
     fold = np.zeros((TAPS, ROWS, 4, ROWS), np.float32)
     for tap in range(TAPS):
         for phase in range(4):
             fold[tap, :, phase, :] = shift[phase_shift(phase, tap)].T
     return (
         shift.reshape(TAPS * ROWS, ROWS),
-        encode.reshape(TAPS * ROWS, 288),
+        encode.reshape(TAPS * ROWS, CELLS),
         fold.reshape(TAPS * ROWS, 4 * ROWS),
-        order.reshape(4 * ROWS, 288),
+        order.reshape(4 * ROWS, CELLS),
     )
 
 
@@ -81,8 +82,8 @@
 
 def body(
     img, tgt, ker, c_shift, c_encode, c_fold, c_order, out,
-    w_in, x_in, t_in, s_shift, s_encode, s_fold, s_order,
-    wp, feat, act, pre, delta3, zed, target,
+    w_in, raw, x_in, s_shift, s_encode, s_fold, s_order,
+    wp, wt, feat, act, pre, delta3, zed, target,
     h_in, skip_in, g_in, gskip_in, h_out, g_out,
     gx, gh, gd, gz, left, grad, pack, y_buf, y_sum, z_out, z_buf,
     load_sem, hop_send, hop_recv, a_send, a_recv, d_send, d_recv, y_send, y_recv, z_send, z_recv,
@@ -108,15 +109,18 @@
     def load(src, dst, n):
         return pltpu.make_async_copy(src, dst, load_sem.at[n])
 
-    w_load = load(ker, w_in, 0)
-    w_load.start()
+    w_loads = [load(ker.at[0, i * 960:(i + 1) * 960], w_in.at[i * 960:(i + 1) * 960], 5 + i) for i in range(3)]
+    for copy in w_loads:
+        copy.start()
 
     barrier = pltpu.get_barrier_semaphore()
     for k in range(1, 4):
         pl.semaphore_signal(barrier, inc=1, device_id={"section": (sec + k) % 4}, device_id_type=MESH)
         for peer in (x_peer, y_peer, z_peer):
             pl.semaphore_signal(barrier, inc=1, device_id=peer(k)[1], device_id_type=MESH)
-    pl.semaphore_wait(barrier, 12)
+
+    def arrive():
+        pl.semaphore_wait(barrier, 12)
 
     row0 = pl.multiple_of(x * 160, 16)
 
@@ -158,40 +162,63 @@
         for k in range(3):
             left[k, pl.ds(pl.multiple_of(p * ROWS, 16), ROWS), :] = part[k * ROWS:(k + 1) * ROWS]
 
-    def left_encode(p):
-        part = mm(s_encode[pl.ds(row0, 240), :], gx[p]).astype(bf)
-        for k in range(3):
-            left[k, pl.ds(pl.multiple_of(p * ROWS, 16), ROWS), 0:GW] = part[k * ROWS:(k + 1) * ROWS]
+    def lay_out_cells():
+        x_in[...] = jnp.zeros((CELLS, GW), bf)
+        lane = lax.broadcasted_iota(jnp.int32, (12, GW), 1)
+        for n in range(2):
+            for j in range(12):
+                start = j * CH - 64 * (j % 2)
+                part = raw[0, :, n, start:start + GW].astype(f32)
+                if j % 2:
+                    part = pltpu.roll(part, GW - 64, 1)
+                x_in[j * 32 + n * 16:j * 32 + n * 16 + 12, :] = jnp.where(lane < CH, part, 0.0).astype(bf)
+
+    def turn_weights():
+        def one(t, carry):
+            rows = pl.ds(pl.multiple_of(t * GW, 16), GW)
+            for g in range(2):
+                wt[g, rows, :] = wp[g, rows, :].T
+            return carry
+
+        lax.fori_loop(0, TAPS, one, 0)
 
     @pl.when(sec == 0)
     def encoder():
-        loads = [load(img, x_in, 1), load(c_encode, s_encode, 2)]
+        loads = [load(img, raw, 1), load(c_encode, s_encode, 2)]
         for copy in loads:
             copy.start()
         for copy in loads:
             copy.wait()
-        e_all = mm(s_encode[...], x_in[...]).astype(bf)
-        w_load.wait()
+        lay_out_cells()
+        zed[:, 0:GW] = mm(s_encode[...], x_in[...]).astype(bf)
         acc = jnp.zeros((ROWS, 2 * CH), f32)
         for t in range(TAPS):
-            acc = acc + mm(e_all[t * ROWS:(t + 1) * ROWS, 0:CH], w_in[t * CH:(t + 1) * CH, :])
+            if t % 3 == 0:
+                w_loads[t // 3].wait()
+            acc = acc + mm(zed[t * ROWS:(t + 1) * ROWS, 0:CH], w_in[t * CH:(t + 1) * CH, :])
         wide = jnp.concatenate([acc, jnp.zeros((ROWS, 128), f32)], axis=1)
         moved = pltpu.roll(wide, 64, 1)
         lane = lax.broadcasted_iota(jnp.int32, (ROWS, 2 * GW), 1)
         wide = jnp.where(lane < CH, wide, jnp.where((lane >= GW) & (lane < GW + CH), moved, 0.0))
         act[...] = wide
         h_out[...] = silu(wide).astype(bf)
+        arrive()
         sends = [
             remote(h_out, h_in, hop_send.at[0], hop_recv.at[0], {"section": 1}),
             remote(h_out, skip_in, hop_send.at[1], hop_recv.at[1], {"section": 3}),
         ]
         for copy in sends:
             copy.start()
-        sends += gather_start(x_in, gx, a_send, a_recv)
-        gx[x] = x_in[...]
-        left_encode(x)
-        for k in range(1, 4):
-            left_encode(gather_wait(k, x_in, gx, a_send, a_recv))
+        for k in range(1, 4):
+            p, dev = x_peer(k)
+            rows = pl.ds(pl.multiple_of(p * 160, 16), 240)
+            copy = remote(zed.at[rows, 0:GW], gx.at[x], a_send.at[p], a_recv.at[x], dev)
+            copy.start()
+            sends.append(copy)
+        gx[x] = zed[pl.ds(row0, 240), 0:GW]
+        for k in range(1, 4):
+            p, dev = x_peer(k)
+            remote(zed.at[0:240, 0:GW], gx.at[p], a_send.at[p], a_recv.at[p], dev).wait_recv()
         remote(g_out, gskip_in, hop_send.at[3], hop_recv.at[3], {"section": 3}).wait_recv()
         remote(g_out, g_in, hop_send.at[2], hop_recv.at[2], {"section": 1}).wait_recv()
         total = g_in[...].astype(f32) + gskip_in[...].astype(f32)
@@ -202,7 +229,8 @@
             gather_wait(k, h_in, gd, d_send, d_recv)
         right = gd[...].reshape(4 * ROWS, 2 * GW)
         for k in range(3):
-            grad[k * CH:(k + 1) * CH, :] = mm_tn(left[k, :, 0:GW], right)[0:CH]
+            lhs = gx[:, k * ROWS:(k + 1) * ROWS, :].reshape(4 * ROWS, GW)
+            grad[k * CH:(k + 1) * CH, :] = mm_tn(lhs, right)[0:CH]
         for copy in sends:
             copy.wait_send()
 
@@ -210,9 +238,11 @@
     def centre():
         s_load = load(c_shift, s_shift, 1)
         s_load.start()
-        w_load.wait()
+        for copy in w_loads:
+            copy.wait()
         pack_weights()
         s_load.wait()
+        arrive()
         remote(h_out, h_in, hop_send.at[0], hop_recv.at[0], {"section": sec - 1}).wait_recv()
         h = h_in[...]
         shifted = mm(s_shift[...], h).astype(bf)
@@ -230,6 +260,7 @@
         left_shift(x)
         for k in range(1, 4):
             left_shift(gather_wait(k, h_in, gh, a_send, a_recv))
+        turn_weights()
         remote(g_out, g_in, hop_send.at[2], hop_recv.at[2], {"section": sec + 1}).wait_recv()
         delta = (g_in[...].astype(f32) * silu_slope(act[...])).astype(bf)
         skip_in[...] = delta
@@ -239,7 +270,7 @@
             acc = g_in[:, group(g)].astype(f32)
             for t in range(TAPS):
                 piece = back[(8 - t) * ROWS:(9 - t) * ROWS, group(g)]
-                acc = acc + mm_nt(piece, wp[g, t * GW:(t + 1) * GW, :])
+                acc = acc + mm(piece, wt[g, t * GW:(t + 1) * GW, :])
             g_out[:, group(g)] = acc.astype(bf)
         hop = remote(g_out, g_in, hop_send.at[2], hop_recv.at[2], {"section": sec - 1})
         hop.start()
@@ -256,14 +287,18 @@
 
     @pl.when(sec == 3)
     def decoder():
-        loads = [load(c_shift, s_shift, 1), load(c_fold, s_fold, 2), load(c_order, s_order, 3), load(tgt, t_in, 4)]
+        loads = [load(c_shift, s_shift, 1), load(c_fold, s_fold, 2), load(c_order, s_order, 3), load(tgt, raw, 4)]
         for copy in loads:
             copy.start()
-        w_load.wait()
+        for copy in w_loads:
+            copy.wait()
         pack_weights()
+        turn_weights()
         for copy in loads:
             copy.wait()
-        target[...] = mm(s_order[...], t_in[...])
+        lay_out_cells()
+        target[...] = mm(s_order[...], x_in[...])
+        arrive()
         remote(h_out, skip_in, hop_send.at[1], hop_recv.at[1], {"section": 0}).wait_recv()
         remote(h_out, h_in, hop_send.at[0], hop_recv.at[0], {"section": 2}).wait_recv()
         u = (h_in[...].astype(f32) + skip_in[...].astype(f32)).astype(bf)
@@ -295,7 +330,7 @@
         for g in range(2):
             acc = jnp.zeros((ROWS, GW), f32)
             for t in range(TAPS):
-                acc = acc + mm_nt(zed[t * ROWS:(t + 1) * ROWS, group(g)], wp[g, t * GW:(t + 1) * GW, :])
+                acc = acc + mm(zed[t * ROWS:(t + 1) * ROWS, group(g)], wt[g, t * GW:(t + 1) * GW, :])
             g_out[:, group(g)] = acc.astype(bf)
         hops = [
             remote(g_out, g_in, hop_send.at[2], hop_recv.at[2], {"section": 2}),
@@ -351,7 +386,7 @@
         p, dev = z_peer(k)
         remote(z_out.at[p], z_buf.at[p], z_send.at[p], z_recv.at[p], dev).wait_recv()
         total = total + z_buf[p].astype(f32)
-    out[...] = total[0:SHARE]
+    out[:, 0, :] = total[0:SHARE]
     for copy in sends:
         copy.wait_send()
 
@@ -359,8 +394,8 @@
 def on_device(images, targets, kernels):
     bf = jnp.bfloat16
 
-    def cells(grids):
-        return jnp.pad(grids.reshape(288, CH), ((0, 0), (0, GW - CH)))
+    def by_rows(grids):
+        return jnp.transpose(grids, (1, 2, 0, 3))
 
     consts = [jnp.asarray(t, bf) for t in tables()]
     vm = pltpu.VMEM
@@ -368,17 +403,18 @@
     hop = vm((ROWS, 2 * GW), bf)
     result = pl.pallas_call(
         body,
-        out_shape=jax.ShapeDtypeStruct((SHARE, 2 * CH), jnp.float32),
-        in_specs=[pl.BlockSpec(memory_space=pl.ANY)] * 7,
+        out_shape=jax.ShapeDtypeStruct((SHARE, 1, 2 * CH), jnp.float32),
+        in_specs=[pl.BlockSpec(memory_space=pltpu.HBM)] * 7,
         out_specs=pl.BlockSpec(memory_space=pltpu.VMEM),
         scratch_shapes=[
             vm((TAPS * CH, 2 * CH), bf),
-            vm((288, GW), bf),
-            vm((288, GW), bf),
+            vm((1, 12, 2, 12 * CH), bf),
+            vm((CELLS, GW), bf),
             vm((TAPS * ROWS, ROWS), bf),
-            vm((TAPS * ROWS, 288), bf),
+            vm((TAPS * ROWS, CELLS), bf),
             vm((TAPS * ROWS, 4 * ROWS), bf),
-            vm((4 * ROWS, 288), bf),
+            vm((4 * ROWS, CELLS), bf),
+            vm((2, TAPS * GW, GW), bf),
             vm((2, TAPS * GW, GW), bf),
             vm((2, 4 * ROWS, TAPS * GW), bf),
             vm((ROWS, 2 * GW), jnp.float32),
@@ -387,7 +423,7 @@
             vm((TAPS * ROWS, 2 * GW), bf),
             vm((4 * ROWS, GW), jnp.float32),
             hop, hop, hop, hop, hop, hop,
-            vm((4, 288, GW), bf),
+            vm((4, 240, GW), bf),
             vm((4, ROWS, 2 * GW), bf),
             vm((4, ROWS, 2 * GW), bf),
             vm((4, 240, 2 * GW), bf),
@@ -402,10 +438,10 @@
             dma((4,)), dma((4,)), dma((4,)), dma((4,)), dma((4,)), dma((4,)), dma((4,)), dma((4,)),
         ],
         compiler_params=pltpu.CompilerParams(
-            collective_id=0, has_side_effects=True, vmem_limit_bytes=48 * 1024 * 1024
+            collective_id=0, has_side_effects=True, vmem_limit_bytes=63 * 1024 * 1024
         ),
-    )(cells(images), cells(targets), kernels[0], *consts)
-    return result[None]
+    )(by_rows(images), by_rows(targets), kernels, *consts)
+    return jnp.transpose(result, (1, 0, 2))
 
 
 def solution(mesh):

time: 68.9 us -> 62.7 us (0.910)
  local copies, waits for them, and re-layouts: 9.35 us -> 1.58 us
  Pallas kernels: 59.2 us -> 61 us
    unnamed x12 -> x1, local copies, waits for them, and re-layouts: 7.91 us -> 1.58 us
    pallas_call x1, Pallas kernels: 59.2 us -> 61 us  [on_device(): pl.pallas_call(body, out_shape=jax.ShapeDtypeStruct((SHARE, 1, 2 * CH), j...]
    broadcast_in_dim x1 -> x0, local copies, waits for them, and re-layouts: 0.77 us -> none  [on_device(): return result[None]]
where the time goes in v1:
time: 62.7 us; the launch traced here: 62.6 us
  Pallas kernels  61 us (97%)
  local copies, waits for them, and re-layouts  1.58 us (3%)
    pallas_call x1, Pallas kernels, on_device(): pl.pallas_call(body, out_shape=jax.ShapeDtypeStruct((SHARE, 1, 2 * CH), j...  61 us
    unnamed x1, local copies, waits for them, and re-layouts  1.58 us

profile of v1, /device:TPU:8, one launch (start us, length us, event | category | flops | bytes accessed | tf_op | source)
XLA Modules:
  0.0 62.6 jit_solution(5581504350344973531)
XLA Ops:
  0.0 61.0 %shard_map.73 = f32[45,1,640]{2,1,0:T(1,128)} custom-call(bf16[1,12,2,3840]{3,2,1,0:T(2,128)(2,1)} %bitcast.4, bf16[1,12,2,3840]{3,2,1,0:T(2,128)(2,1)} %bitcast.5, bf16[1,2880,640]{2,1,0:T(8,128)(2,1)} %ker.1, bf16[720,80]{1,0:T(8,128)(2,1)} %constant.8.clone.c_shift, bf16[720,384]{1,0:T(8,128)(2,1)} %constant.9.clone.c_encode, ...), custom_call_target="tpu_custom_call" | custom-call | tf_op jit(solution)/shard_map/pallas_call | solution.py:404
  61.0 1.6 %copy.9 = f32[1,45,640]{2,0,1:T(1,128)} copy(f32[1,45,640]{2,0,1:T(1,128)} %bitcast.3) | data formatting | bytes 230400

commit v2 on v1

v2 whole, which is shorter than its diff:
```python
import jax
import jax.numpy as jnp
import numpy as np
from jax import lax
from jax.experimental import pallas as pl
from jax.experimental.pallas import tpu as pltpu
from jax.sharding import PartitionSpec as P

MESH = pl.DeviceIdType.MESH
ROWS = 80
CH = 320
GW = 384
TAPS = 9
SHARE = 45
SLOT = 48
CELLS = 12 * 32


def phase_shift(phase, tap):
    alpha, beta = divmod(phase, 2)
    a, b = divmod(tap, 3)
    return ((alpha + a - 1) // 2 + 1) * 3 + ((beta + b - 1) // 2 + 1)


def tables():
    shift = np.zeros((TAPS, ROWS, ROWS), np.float32)
    encode = np.zeros((TAPS, ROWS, CELLS), np.float32)
    order = np.zeros((4, ROWS, CELLS), np.float32)
    for n in range(2):
        for i in range(6):
            for j in range(6):
                r = n * 36 + i * 6 + j
                for tap in range(TAPS):
                    a, b = divmod(tap, 3)
                    ii, jj = i + a - 1, j + b - 1
                    if 0 <= ii < 6 and 0 <= jj < 6:
                        shift[tap, r, n * 36 + ii * 6 + jj] = 1
                    ii, jj = 2 * i + a - 1, 2 * j + b - 1
                    if 0 <= ii < 12 and 0 <= jj < 12:
                        encode[tap, r, jj * 32 + n * 16 + ii] = 1
                for phase in range(4):
                    alpha, beta = divmod(phase, 2)
                    order[phase, r, (2 * j + beta) * 32 + n * 16 + 2 * i + alpha] = 1
    fold = np.zeros((TAPS, ROWS, 4, ROWS), np.float32)
    for tap in range(TAPS):
        for phase in range(4):
            fold[tap, :, phase, :] = shift[phase_shift(phase, tap)].T
    return (
        shift.reshape(TAPS * ROWS, ROWS),
        encode.reshape(TAPS * ROWS, CELLS),
        fold.reshape(TAPS * ROWS, 4 * ROWS),
        order.reshape(4 * ROWS, CELLS),
    )


def silu(v):
    return v * jax.nn.sigmoid(v)


def silu_slope(v):
    g = jax.nn.sigmoid(v)
    return g * (1.0 + v * (1.0 - g))


def mm(a, b):
    return jnp.dot(a, b, preferred_element_type=jnp.float32)


def mm_nt(a, b):
    return lax.dot_general(a, b, (((1,), (1,)), ((), ())), preferred_element_type=jnp.float32)


def remote(src, dst, send_sem, recv_sem, device):
    return pltpu.make_async_remote_copy(
        src_ref=src, dst_ref=dst, send_sem=send_sem, recv_sem=recv_sem, device_id=device, device_id_type=MESH
    )


def body(
    img, tgt, ker, c_shift, c_encode, c_fold, c_order, out,
    w_in, raw, x_in, s_shift, s_encode, s_fold, s_order,
    wp, wt, feat, act, pre, target, zed,
    h_in, skip_in, g_in, gskip_in, h_out, g_out,
    gx, gh, gd, gd3, taps, select, left, pack, r_buf, r_sum, z_out, z_buf,
    load_sem, hop_send, hop_recv, a_send, a_recv, d_send, d_recv, r_send, r_recv, z_send, z_recv,
):
    bf = jnp.bfloat16
    f32 = jnp.float32
    sec = lax.axis_index("section")
    dp = lax.axis_index("dp")
    x, y, z = dp // 16, (dp // 4) % 4, dp % 4

    def x_peer(k):
        return {"dp": (x + k) % 4 * 16 + y * 4 + z}

    def y_peer(k):
        return {"dp": x * 16 + (y + k) % 4 * 4 + z}

    def z_peer(k):
        return {"dp": x * 16 + y * 4 + (z + k) % 4}

    gather_peer = (x_peer, y_peer)
    reduce_peer = (y_peer, x_peer)

    def load(src, dst, n):
        return pltpu.make_async_copy(src, dst, load_sem.at[n])

    w_loads = []
    for n, (first, last) in enumerate(((0, GW), (GW, 2 * CH))):
        for i in range(3):
            part = (slice(i * 960, (i + 1) * 960), slice(first, last))
            w_loads.append(load(ker.at[(0, *part)], w_in.at[part], 4 + 3 * n + i))
    x_load = load(img, raw, 0)
    e_load = load(c_encode, s_encode, 1)

    @pl.when(sec == 0)
    def first_loads():
        x_load.start()
        e_load.start()

    for copy in w_loads:
        copy.start()

    barrier = pltpu.get_barrier_semaphore()
    for k in range(1, 4):
        pl.semaphore_signal(barrier, inc=1, device_id={"section": (sec + k) % 4}, device_id_type=MESH)
        for peer in (x_peer, y_peer, z_peer):
            pl.semaphore_signal(barrier, inc=1, device_id=peer(k), device_id_type=MESH)

    def arrive():
        pl.semaphore_wait(barrier, 12)

    def spread(src, buf, send, recv, g):
        copies = []
        for k in (1, 3, 2):
            copy = remote(src, buf.at[g, 4 - k], send.at[g, k], recv.at[g, 4 - k], gather_peer[g](k))
            copy.start()
            copies.append(copy)
        return copies

    def spread_wait(src, buf, send, recv, g, k):
        remote(src, buf.at[g, k], send.at[g, k], recv.at[g, k], gather_peer[g](k)).wait_recv()

    def hop(kind, src, dst, g, to):
        return remote(src.at[g], dst.at[g], hop_send.at[kind, g], hop_recv.at[kind, g], {"section": to})

    def rows_of(t, n=ROWS):
        return slice(t * n, (t + 1) * n)

    def pack_weights():
        lane = lax.broadcasted_iota(jnp.int32, (CH, GW), 1)

        def one(t, carry):
            rows = pl.ds(pl.multiple_of(t * CH, 16), CH)
            base = pl.multiple_of(t * GW, 16)
            first = w_in[rows, 0:GW].astype(f32)
            wp[0, pl.ds(base, CH), :] = jnp.where(lane < CH, first, 0.0).astype(bf)
            second = pltpu.roll(w_in[rows, 256:640].astype(f32), GW - 64, 1)
            wp[1, pl.ds(base, CH), :] = jnp.where(lane < CH, second, 0.0).astype(bf)
            for g in range(2):
                wp[g, pl.ds(base + CH, GW - CH), :] = jnp.zeros((GW - CH, GW), bf)
            return carry

        lax.fori_loop(0, TAPS, one, 0)

    def turn_weights():
        def one(t, carry):
            rows = pl.ds(pl.multiple_of(t * GW, 16), GW)
            for g in range(2):
                wt[g, rows, :] = wp[g, rows, :].T
            return carry

        lax.fori_loop(0, TAPS, one, 0)

    def lay_out_cells():
        x_in[...] = jnp.zeros((CELLS, GW), bf)
        lane = lax.broadcasted_iota(jnp.int32, (12, GW), 1)
        for n in range(2):
            for j in range(12):
                start = j * CH - 64 * (j % 2)
                part = raw[0, :, n, start:start + GW].astype(f32)
                if j % 2:
                    part = pltpu.roll(part, GW - 64, 1)
                x_in[j * 32 + n * 16:j * 32 + n * 16 + 12, :] = jnp.where(lane < CH, part, 0.0).astype(bf)

    def make_select():
        lane = lax.broadcasted_iota(jnp.int32, (SLOT, GW), 1)
        row = lax.broadcasted_iota(jnp.int32, (SLOT, GW), 0)
        for j in range(4):
            value = row - lane + SHARE * ((z + j) % 4)
            select[rows_of(j, SLOT), :] = jnp.where((row < SHARE) & (lane < CH), value, -100000)

    def block_start(g, k):
        return 720 * x + 180 * ((y + k) % 4) if g == 0 else 720 * ((x + k) % 4) + 180 * y

    def block_tap(g, k, i):
        return jnp.minimum(block_start(g, k) // CH + i, TAPS - 1)

    def block_rows(g, k, i, source):
        start = block_start(g, k)
        chosen = select[...] == CH * (start // CH + i) - start
        return mm_nt(jnp.where(chosen, 1.0, 0.0).astype(bf), source)

    def make_left(g):
        for k in range(4):
            rows = sum(block_rows(g, k, i, taps[block_tap(g, k, i)]) for i in range(2))
            left[0, g, rows_of(k, 4 * SLOT), :] = rows.astype(bf)

    def fill_taps(k, table, source):
        part = mm(table, source).astype(bf)
        for t in range(TAPS):
            taps[t, rows_of(k), :] = part[rows_of(t)]

    def hand_block(g, k, block):
        if k == 0:
            r_sum[g] = block
            return []
        pack[g, k] = block.astype(bf)
        copy = remote(pack.at[g, k], r_buf.at[g, 4 - k], r_send.at[g, k], r_recv.at[g, 4 - k], reduce_peer[g](k))
        copy.start()
        return [copy]

    def gradient(g):
        copies = []
        for k in (1, 3, 2):
            spread_wait(gd.at[g, 0], gd, d_send, d_recv, g, k)
        right = gd[g].reshape(4 * ROWS, GW)
        for k in (2, 1, 3, 0):
            copies += hand_block(g, k, mm(left[0, g, rows_of(k, 4 * SLOT), :], right))
        return copies

    @pl.when(sec == 0)
    def encoder():
        x_load.wait()
        lay_out_cells()
        e_load.wait()
        zed[...] = mm(s_encode[...], x_in[...]).astype(bf)
        lane = lax.broadcasted_iota(jnp.int32, (ROWS, GW), 1)
        sends = []
        for g in range(2):
            acc = jnp.zeros((ROWS, GW), f32)
            for t in range(TAPS):
                if t % 3 == 0:
                    w_loads[3 * g + t // 3].wait()
                acc = acc + mm(zed[rows_of(t), 0:CH], w_in[rows_of(t, CH), g * 256:g * 256 + GW])
            if g:
                acc = pltpu.roll(acc, GW - 64, 1)
            acc = jnp.where(lane < CH, acc, 0.0)
            act[g] = acc
            h_out[g] = silu(acc).astype(bf)
            if g == 0:
                arrive()
            for copy in (hop(0, h_out, h_in, g, 1), hop(1, h_out, skip_in, g, 3)):
                copy.start()
                sends.append(copy)
        for g in range(2):
            sends += spread(x_in, gx, a_send, a_recv, g)
        make_select()
        for g in range(2):
            for t in range(TAPS):
                taps[t, rows_of(0), :] = zed[rows_of(t)]
            for k in (1, 3, 2):
                spread_wait(x_in, gx, a_send, a_recv, g, k)
                fill_taps(k, s_encode[...], gx[g, k])
            make_left(g)
        for g in range(2):
            hop(3, g_out, gskip_in, g, 3).wait_recv()
            hop(2, g_out, g_in, g, 1).wait_recv()
            total = g_in[g].astype(f32) + gskip_in[g].astype(f32)
            gd[g, 0] = (total * silu_slope(act[g])).astype(bf)
            sends += spread(gd.at[g, 0], gd, d_send, d_recv, g)
        for g in range(2):
            sends += gradient(g)
        for copy in sends:
            copy.wait_send()

    @pl.when((sec == 1) | (sec == 2))
    def centre():
        s_load = load(c_shift, s_shift, 2)
        s_load.start()
        for copy in w_loads:
            copy.wait()
        pack_weights()
        s_load.wait()

        @pl.when(sec == 2)
        def turn_early():
            turn_weights()

        arrive()
        sends = []
        for g in range(2):
            hop(0, h_out, h_in, g, sec - 1).wait_recv()
            shifted = mm(s_shift[...], h_in[g]).astype(bf)
            acc = jnp.zeros((ROWS, GW), f32)
            for t in range(TAPS):
                acc = acc + mm(shifted[rows_of(t)], wp[g, rows_of(t, GW), :])
            act[g] = acc
            h_out[g] = (h_in[g].astype(f32) + silu(acc)).astype(bf)
            copy = hop(0, h_out, h_in, g, sec + 1)
            copy.start()
            sends.append(copy)
        for g in range(2):
            sends += spread(h_in.at[g], gh, a_send, a_recv, g)

        @pl.when(sec == 1)
        def turn_late():
            turn_weights()

        make_select()

        def prepare(g):
            fill_taps(0, s_shift[...], h_in[g])
            for k in (1, 3, 2):
                spread_wait(h_in.at[g], gh, a_send, a_recv, g, k)
                fill_taps(k, s_shift[...], gh[g, k])
            make_left(g)

        prepare(0)

        @pl.when(sec == 1)
        def prepare_early():
            prepare(1)

        for g in range(2):
            hop(2, g_out, g_in, g, sec + 1).wait_recv()
            delta = (g_in[g].astype(f32) * silu_slope(act[g])).astype(bf)
            gd[g, 0] = delta
            back = mm(s_shift[...], delta).astype(bf)
            acc = g_in[g].astype(f32)
            for t in range(TAPS):
                acc = acc + mm(back[rows_of(8 - t)], wt[g, rows_of(t, GW), :])
            g_out[g] = acc.astype(bf)
            copy = hop(2, g_out, g_in, g, sec - 1)
            copy.start()
            sends.append(copy)
            sends += spread(gd.at[g, 0], gd, d_send, d_recv, g)

        @pl.when(sec == 2)
        def prepare_late():
            prepare(1)

        for g in range(2):
            sends += gradient(g)
        for copy in sends:
            copy.wait_send()

    @pl.when(sec == 3)
    def decoder():
        loads = [load(c_shift, s_shift, 2), load(c_fold, s_fold, 3), load(c_order, s_order, 1), load(tgt, raw, 0)]
        for copy in loads:
            copy.start()
        for copy in w_loads:
            copy.wait()
        pack_weights()
        turn_weights()
        for copy in loads:
            copy.wait()
        lay_out_cells()
        target[...] = mm(s_order[...], x_in[...])
        make_select()
        arrive()
        sends = []
        for g in range(2):
            hop(1, h_out, skip_in, g, 0).wait_recv()
            hop(0, h_out, h_in, g, 2).wait_recv()
            u = (h_in[g].astype(f32) + skip_in[g].astype(f32)).astype(bf)
            gh[g, 0] = u
            sends += spread(gh.at[g, 0], gh, a_send, a_recv, g)
            shifted = mm(s_shift[...], u).astype(bf)
            for phase in range(4):
                for t in range(TAPS):
                    feat[g, rows_of(phase), rows_of(t, GW)] = shifted[rows_of(phase_shift(phase, t))]
            pre[g] = mm(feat[g], wp[g])
        value, gate = pre[0], pre[1]
        sig = jax.nn.sigmoid(gate)
        act_gate = gate * sig
        residual = (value * act_gate - target[...]) * (1.0 / 128.0)
        gd3[0, 0] = (residual * act_gate).astype(bf)
        gd3[1, 0] = (residual * value * (sig * (1.0 + gate * (1.0 - sig)))).astype(bf)
        for g in range(2):
            sends += spread(gd3.at[g, 0], gd3, d_send, d_recv, g)
        for g in range(2):
            back = mm(s_fold[...], gd3[g, 0]).astype(bf)
            acc = jnp.zeros((ROWS, GW), f32)
            for t in range(TAPS):
                acc = acc + mm(back[rows_of(t)], wt[g, rows_of(t, GW), :])
            g_out[g] = acc.astype(bf)
            for copy in (hop(2, g_out, g_in, g, 2), hop(3, g_out, gskip_in, g, 0)):
                copy.start()
                sends.append(copy)
        for g in range(2):
            for k in (1, 3, 2):
                spread_wait(gh.at[g, 0], gh, a_send, a_recv, g, k)
            source = gh[g].reshape(4 * ROWS, GW)
            for k in range(4):
                for i in range(2):
                    left[i, g, rows_of(k, 4 * SLOT), :] = block_rows(g, k, i, source).astype(bf)
        for g in range(2):
            fill_taps(0, s_fold[...], gd3[g, 0])
            for k in (1, 3, 2):
                spread_wait(gd3.at[g, 0], gd3, d_send, d_recv, g, k)
                fill_taps(k, s_fold[...], gd3[g, k])
            for k in (2, 1, 3, 0):
                block = sum(mm(left[i, g, rows_of(k, 4 * SLOT), :], taps[block_tap(g, k, i)]) for i in range(2))
                sends += hand_block(g, k, block)
        for copy in sends:
            copy.wait_send()

    sends = []
    for g in range(2):
        for k in (1, 3, 2):
            remote(pack.at[g, k], r_buf.at[g, k], r_send.at[g, k], r_recv.at[g, k], reduce_peer[g](k)).wait_recv()
        r_sum[g] = r_sum[g] + r_buf[g, 1].astype(f32) + r_buf[g, 2].astype(f32) + r_buf[g, 3].astype(f32)
        z_out[g] = r_sum[g].astype(bf)
        for k in (2, 1, 3):
            copy = remote(z_out.at[g, rows_of(k, SLOT)], z_buf.at[g, 4 - k], z_send.at[g, k], z_recv.at[g, 4 - k], z_peer(k))
            copy.start()
            sends.append(copy)
    halves = []
    for g in range(2):
        total = r_sum[g, 0:SLOT, :]
        for k in (1, 3, 2):
            remote(z_out.at[g, rows_of(k, SLOT)], z_buf.at[g, k], z_send.at[g, k], z_recv.at[g, k], z_peer(k)).wait_recv()
            total = total + z_buf[g, k].astype(f32)
        halves.append(jnp.concatenate([total, jnp.zeros((SLOT, 256), f32)], axis=1))
    whole = halves[0] + pltpu.roll(halves[1], CH, 1)
    out[:, 0, :] = whole[0:SHARE]
    for copy in sends:
        copy.wait_send()


def on_device(images, targets, kernels):
    bf = jnp.bfloat16

    def by_rows(grids):
        return jnp.transpose(grids, (1, 2, 0, 3))

    consts = [jnp.asarray(t, bf) for t in tables()]
    vm = pltpu.VMEM
    dma = pltpu.SemaphoreType.DMA
    hop = vm((2, ROWS, GW), bf)
    result = pl.pallas_call(
        body,
        out_shape=jax.ShapeDtypeStruct((SHARE, 1, 2 * CH), jnp.float32),
        in_specs=[pl.BlockSpec(memory_space=pltpu.HBM)] * 7,
        out_specs=pl.BlockSpec(memory_space=pltpu.VMEM),
        scratch_shapes=[
            vm((TAPS * CH, 2 * CH), bf),
            vm((1, 12, 2, 12 * CH), bf),
            vm((CELLS, GW), bf),
            vm((TAPS * ROWS, ROWS), bf),
            vm((TAPS * ROWS, CELLS), bf),
            vm((TAPS * ROWS, 4 * ROWS), bf),
            vm((4 * ROWS, CELLS), bf),
            vm((2, TAPS * GW, GW), bf),
            vm((2, TAPS * GW, GW), bf),
            vm((2, 4 * ROWS, TAPS * GW), bf),
            vm((2, ROWS, GW), jnp.float32),
            vm((2, 4 * ROWS, GW), jnp.float32),
            vm((4 * ROWS, GW), jnp.float32),
            vm((TAPS * ROWS, GW), bf),
            hop, hop, hop, hop, hop, hop,
            vm((2, 4, CELLS, GW), bf),
            vm((2, 4, ROWS, GW), bf),
            vm((2, 4, ROWS, GW), bf),
            vm((2, 4, 4 * ROWS, GW), bf),
            vm((TAPS, 4 * ROWS, GW), bf),
            vm((4 * SLOT, GW), jnp.int32),
            vm((2, 2, 16 * SLOT, 4 * ROWS), bf),
            vm((2, 4, 4 * SLOT, GW), bf),
            vm((2, 4, 4 * SLOT, GW), bf),
            vm((2, 4 * SLOT, GW), jnp.float32),
            vm((2, 4 * SLOT, GW), bf),
            vm((2, 4, SLOT, GW), bf),
            dma((10,)), dma((4, 2)), dma((4, 2)),
            dma((2, 4)), dma((2, 4)), dma((2, 4)), dma((2, 4)), dma((2, 4)), dma((2, 4)), dma((2, 4)), dma((2, 4)),
        ],
        compiler_params=pltpu.CompilerParams(
            collective_id=0, has_side_effects=True, vmem_limit_bytes=63 * 1024 * 1024
        ),
    )(by_rows(images), by_rows(targets), kernels, *consts)
    return jnp.transpose(result, (1, 0, 2))


def solution(mesh):
    return jax.shard_map(
        on_device,
        mesh=mesh,
        in_specs=(P(None, "dp", None, None), P(None, "dp", None, None), P("section", None, None)),
        out_specs=P("section", "dp", None),
        check_vma=False,
    )
```

time: 62.7 us -> 52.1 us (0.83)
  Pallas kernels: 61 us -> 50 us
    pallas_call x1, Pallas kernels: 61 us -> 50 us  [on_device(): pl.pallas_call(body, out_shape=jax.ShapeDtypeStruct((SHARE, 1, 2 * CH), j...]
where the time goes in v2:
time: 52.1 us; the launch traced here: 51.6 us
  Pallas kernels  50 us (96%)
  local copies, waits for them, and re-layouts  1.58 us (3%)
    pallas_call x1, Pallas kernels, on_device(): pl.pallas_call(body, out_shape=jax.ShapeDtypeStruct((SHARE, 1, 2 * CH), j...  50 us
    unnamed x1, local copies, waits for them, and re-layouts  1.58 us

profile of v2, /device:TPU:8, one launch (start us, length us, event | category | flops | bytes accessed | tf_op | source)
XLA Modules:
  0.0 51.6 jit_solution(14080308791394085592)
XLA Ops:
  0.0 50.0 %shard_map.73 = f32[45,1,640]{2,1,0:T(1,128)} custom-call(bf16[1,12,2,3840]{3,2,1,0:T(2,128)(2,1)} %bitcast.4, bf16[1,12,2,3840]{3,2,1,0:T(2,128)(2,1)} %bitcast.5, bf16[1,2880,640]{2,1,0:T(8,128)(2,1)} %ker.1, bf16[720,80]{1,0:T(8,128)(2,1)} %constant.8.clone.c_shift, bf16[720,384]{1,0:T(8,128)(2,1)} %constant.9.clone.c_encode, ...), custom_call_target="tpu_custom_call" | custom-call | tf_op jit(solution)/shard_map/pallas_call | solution.py:443
  50.0 1.6 %copy.9 = f32[1,45,640]{2,0,1:T(1,128)} copy(f32[1,45,640]{2,0,1:T(1,128)} %bitcast.3) | data formatting | bytes 230400

commit v3 on v2

--- a/solution.py
+++ b/solution.py
@@ -211,11 +211,27 @@
         for t in range(TAPS):
             taps[t, rows_of(k), :] = part[rows_of(t)]
 
+    def half_lanes(first, second):
+        return jnp.where(lax.broadcasted_iota(jnp.int32, first.shape, 1) < 64, first, pltpu.roll(second, 64, 1))
+
+    def squeeze(block):
+        last = [block[rows_of(j, SLOT), 256:GW] for j in range(4)]
+        side = jnp.concatenate([half_lanes(last[0], last[1]), half_lanes(last[2], last[3])], axis=1)
+        return jnp.concatenate([block[:, 0:256], side], axis=0)
+
+    def z_slot(j):
+        side = slice(4 * SLOT, 5 * SLOT), slice(128 * (j // 2), 128 * (j // 2) + 128)
+        first, second = r_sum[(0, *side)], r_sum[(1, *side)]
+        if j % 2:
+            first = pltpu.roll(first, 64, 1)
+            second = pltpu.roll(second, 64, 1)
+        return jnp.concatenate([r_sum[0, rows_of(j, SLOT), :], r_sum[1, rows_of(j, SLOT), :], half_lanes(first, second)], axis=1)
+
     def hand_block(g, k, block):
         if k == 0:
-            r_sum[g] = block
+            r_sum[g] = squeeze(block)
             return []
-        pack[g, k] = block.astype(bf)
+        pack[g, k] = squeeze(block).astype(bf)
         copy = remote(pack.at[g, k], r_buf.at[g, 4 - k], r_send.at[g, k], r_recv.at[g, 4 - k], reduce_peer[g](k))
         copy.start()
         return [copy]
@@ -316,11 +332,10 @@
                 fill_taps(k, s_shift[...], gh[g, k])
             make_left(g)
 
-        prepare(0)
-
         @pl.when(sec == 1)
         def prepare_early():
-            prepare(1)
+            for g in range(2):
+                prepare(g)
 
         for g in range(2):
             hop(2, g_out, g_in, g, sec + 1).wait_recv()
@@ -338,7 +353,8 @@
 
         @pl.when(sec == 2)
         def prepare_late():
-            prepare(1)
+            for g in range(2):
+                prepare(g)
 
         for g in range(2):
             sends += gradient(g)
@@ -412,20 +428,20 @@
         for k in (1, 3, 2):
             remote(pack.at[g, k], r_buf.at[g, k], r_send.at[g, k], r_recv.at[g, k], reduce_peer[g](k)).wait_recv()
         r_sum[g] = r_sum[g] + r_buf[g, 1].astype(f32) + r_buf[g, 2].astype(f32) + r_buf[g, 3].astype(f32)
-        z_out[g] = r_sum[g].astype(bf)
-        for k in (2, 1, 3):
-            copy = remote(z_out.at[g, rows_of(k, SLOT)], z_buf.at[g, 4 - k], z_send.at[g, k], z_recv.at[g, 4 - k], z_peer(k))
-            copy.start()
-            sends.append(copy)
-    halves = []
-    for g in range(2):
-        total = r_sum[g, 0:SLOT, :]
-        for k in (1, 3, 2):
-            remote(z_out.at[g, rows_of(k, SLOT)], z_buf.at[g, k], z_send.at[g, k], z_recv.at[g, k], z_peer(k)).wait_recv()
-            total = total + z_buf[g, k].astype(f32)
-        halves.append(jnp.concatenate([total, jnp.zeros((SLOT, 256), f32)], axis=1))
-    whole = halves[0] + pltpu.roll(halves[1], CH, 1)
-    out[:, 0, :] = whole[0:SHARE]
+    for k in (2, 1, 3):
+        z_out[k] = z_slot(k).astype(bf)
+        copy = remote(z_out.at[k], z_buf.at[4 - k], z_send.at[k], z_recv.at[4 - k], z_peer(k))
+        copy.start()
+        sends.append(copy)
+    total = z_slot(0)
+    for k in (1, 3, 2):
+        remote(z_out.at[k], z_buf.at[k], z_send.at[k], z_recv.at[k], z_peer(k)).wait_recv()
+        total = total + z_buf[k].astype(f32)
+    lane = lax.broadcasted_iota(jnp.int32, (SLOT, GW), 1)
+    side = total[:, 512:640]
+    moved = pltpu.roll(jnp.concatenate([total[:, 256:512], side], axis=1), 64, 1)
+    upper = jnp.where((lane < 64) | (lane >= CH), jnp.concatenate([side, side, side], axis=1), moved)
+    out[:, 0, :] = jnp.concatenate([total[:, 0:256], upper], axis=1)[0:SHARE]
     for copy in sends:
         copy.wait_send()
 
@@ -468,13 +484,13 @@
             vm((TAPS, 4 * ROWS, GW), bf),
             vm((4 * SLOT, GW), jnp.int32),
             vm((2, 2, 16 * SLOT, 4 * ROWS), bf),
-            vm((2, 4, 4 * SLOT, GW), bf),
-            vm((2, 4, 4 * SLOT, GW), bf),
-            vm((2, 4 * SLOT, GW), jnp.float32),
-            vm((2, 4 * SLOT, GW), bf),
-            vm((2, 4, SLOT, GW), bf),
+            vm((2, 4, 5 * SLOT, 256), bf),
+            vm((2, 4, 5 * SLOT, 256), bf),
+            vm((2, 5 * SLOT, 256), jnp.float32),
+            vm((4, SLOT, 2 * CH), bf),
+            vm((4, SLOT, 2 * CH), bf),
             dma((10,)), dma((4, 2)), dma((4, 2)),
-            dma((2, 4)), dma((2, 4)), dma((2, 4)), dma((2, 4)), dma((2, 4)), dma((2, 4)), dma((2, 4)), dma((2, 4)),
+            dma((2, 4)), dma((2, 4)), dma((2, 4)), dma((2, 4)), dma((2, 4)), dma((2, 4)), dma((4,)), dma((4,)),
         ],
         compiler_params=pltpu.CompilerParams(
             collective_id=0, has_side_effects=True, vmem_limit_bytes=63 * 1024 * 1024

time: 52.1 us -> 50 us (0.960)
  Pallas kernels: 50 us -> 48.3 us
    pallas_call x1, Pallas kernels: 50 us -> 48.3 us  [on_device(): pl.pallas_call(body, out_shape=jax.ShapeDtypeStruct((SHARE, 1, 2 * CH), j...]
where the time goes in v3:
time: 50 us; the launch traced here: 49.9 us
  Pallas kernels  48.3 us (97%)
  local copies, waits for them, and re-layouts  1.58 us (3%)
    pallas_call x1, Pallas kernels, on_device(): pl.pallas_call(body, out_shape=jax.ShapeDtypeStruct((SHARE, 1, 2 * CH), j...  48.3 us
    unnamed x1, local copies, waits for them, and re-layouts  1.58 us

profile of v3, /device:TPU:8, one launch (start us, length us, event | category | flops | bytes accessed | tf_op | source)
XLA Modules:
  0.0 49.9 jit_solution(13381633086388647072)
XLA Ops:
  0.0 48.3 %shard_map.73 = f32[45,1,640]{2,1,0:T(1,128)} custom-call(bf16[1,12,2,3840]{3,2,1,0:T(2,128)(2,1)} %bitcast.4, bf16[1,12,2,3840]{3,2,1,0:T(2,128)(2,1)} %bitcast.5, bf16[1,2880,640]{2,1,0:T(8,128)(2,1)} %ker.1, bf16[720,80]{1,0:T(8,128)(2,1)} %constant.8.clone.c_shift, bf16[720,384]{1,0:T(8,128)(2,1)} %constant.9.clone.c_encode, ...), custom_call_target="tpu_custom_call" | custom-call | tf_op jit(solution)/shard_map/pallas_call | solution.py:459
  48.3 1.6 %copy.9 = f32[1,45,640]{2,0,1:T(1,128)} copy(f32[1,45,640]{2,0,1:T(1,128)} %bitcast.3) | data formatting | bytes 230400

commit v4 on v3

--- a/solution.py
+++ b/solution.py
@@ -81,8 +81,9 @@
     w_in, raw, x_in, s_shift, s_encode, s_fold, s_order,
     wp, wt, feat, act, pre, target, zed,
     h_in, skip_in, g_in, gskip_in, h_out, g_out,
-    gx, gh, gd, gd3, taps, select, left, pack, r_buf, r_sum, z_out, z_buf,
-    load_sem, hop_send, hop_recv, a_send, a_recv, d_send, d_recv, r_send, r_recv, z_send, z_recv,
+    gx, gh, gd, gd3, g_act, g_skip, g_back, taps, select, left, pack, r_buf, r_sum, z_out, z_buf,
+    load_sem, hop_send, hop_recv, a_send, a_recv, d_send, d_recv, c_send, c_recv, s_send, s_recv, b_send, b_recv,
+    r_send, r_recv, z_send, z_recv,
 ):
     bf = jnp.bfloat16
     f32 = jnp.float32
@@ -127,8 +128,14 @@
         for peer in (x_peer, y_peer, z_peer):
             pl.semaphore_signal(barrier, inc=1, device_id=peer(k), device_id_type=MESH)
 
-    def arrive():
-        pl.semaphore_wait(barrier, 12)
+    @pl.when(sec == 0)
+    def greet_senders():
+        for k in range(1, 4):
+            for peer in (x_peer, y_peer):
+                pl.semaphore_signal(barrier, inc=1, device_id={"section": 1, **peer(k)}, device_id_type=MESH)
+
+    def arrive(more=0):
+        pl.semaphore_wait(barrier, 12 + more)
 
     def spread(src, buf, send, recv, g):
         copies = []
@@ -172,13 +179,12 @@
 
         lax.fori_loop(0, TAPS, one, 0)
 
-    def lay_out_cells():
-        x_in[...] = jnp.zeros((CELLS, GW), bf)
+    def lay_out_cells(grids):
         lane = lax.broadcasted_iota(jnp.int32, (12, GW), 1)
         for n in range(2):
             for j in range(12):
                 start = j * CH - 64 * (j % 2)
-                part = raw[0, :, n, start:start + GW].astype(f32)
+                part = grids[0, :, n, start:start + GW].astype(f32)
                 if j % 2:
                     part = pltpu.roll(part, GW - 64, 1)
                 x_in[j * 32 + n * 16:j * 32 + n * 16 + 12, :] = jnp.where(lane < CH, part, 0.0).astype(bf)
@@ -238,8 +244,6 @@
 
     def gradient(g):
         copies = []
-        for k in (1, 3, 2):
-            spread_wait(gd.at[g, 0], gd, d_send, d_recv, g, k)
         right = gd[g].reshape(4 * ROWS, GW)
         for k in (2, 1, 3, 0):
             copies += hand_block(g, k, mm(left[0, g, rows_of(k, 4 * SLOT), :], right))
@@ -247,8 +251,9 @@
 
     @pl.when(sec == 0)
     def encoder():
+        x_in[...] = jnp.zeros((CELLS, GW), bf)
         x_load.wait()
-        lay_out_cells()
+        lay_out_cells(raw)
         e_load.wait()
         zed[...] = mm(s_encode[...], x_in[...]).astype(bf)
         lane = lax.broadcasted_iota(jnp.int32, (ROWS, GW), 1)
@@ -270,22 +275,35 @@
                 copy.start()
                 sends.append(copy)
         for g in range(2):
-            sends += spread(x_in, gx, a_send, a_recv, g)
+            sends += spread(raw, gx, a_send, a_recv, g)
+        for g in range(2):
+            sends += spread(act.at[g], g_act, c_send, c_recv, g)
         make_select()
         for g in range(2):
             for t in range(TAPS):
                 taps[t, rows_of(0), :] = zed[rows_of(t)]
             for k in (1, 3, 2):
-                spread_wait(x_in, gx, a_send, a_recv, g, k)
-                fill_taps(k, s_encode[...], gx[g, k])
+                spread_wait(raw, gx, a_send, a_recv, g, k)
+                lay_out_cells(gx.at[g, k])
+                fill_taps(k, s_encode[...], x_in[...])
             make_left(g)
         for g in range(2):
             hop(3, g_out, gskip_in, g, 3).wait_recv()
-            hop(2, g_out, g_in, g, 1).wait_recv()
-            total = g_in[g].astype(f32) + gskip_in[g].astype(f32)
-            gd[g, 0] = (total * silu_slope(act[g])).astype(bf)
-            sends += spread(gd.at[g, 0], gd, d_send, d_recv, g)
-        for g in range(2):
+            sends += spread(gskip_in.at[g], g_skip, s_send, s_recv, g)
+        for g in range(2):
+            for k in (1, 3, 2):
+                spread_wait(act.at[g], g_act, c_send, c_recv, g, k)
+                spread_wait(gskip_in.at[g], g_skip, s_send, s_recv, g, k)
+        for g in range(2):
+            for k in (0, 1, 3, 2):
+                if k:
+                    remote(g_out.at[g], g_back.at[g, k], b_send.at[g, k], b_recv.at[g, k], gather_peer[g](k)).wait_recv()
+                    pre_k, skip_k = g_act[g, k], g_skip[g, k]
+                else:
+                    remote(g_out.at[g], g_back.at[g, 0], b_send.at[g, 0], b_recv.at[g, 0], {"section": 1}).wait_recv()
+                    pre_k, skip_k = act[g], gskip_in[g]
+                total = g_back[g, k].astype(f32) + skip_k.astype(f32)
+                gd[g, k] = (total * silu_slope(pre_k)).astype(bf)
             sends += gradient(g)
         for copy in sends:
             copy.wait_send()
@@ -303,7 +321,7 @@
         def turn_early():
             turn_weights()
 
-        arrive()
+        arrive(jnp.where(sec == 1, 6, 0))
         sends = []
         for g in range(2):
             hop(0, h_out, h_in, g, sec - 1).wait_recv()
@@ -325,6 +343,13 @@
 
         make_select()
 
+        def to_encoders(g):
+            copies = []
+            for k in (1, 3, 2, 0):
+                to = {"section": 0, **gather_peer[g](k)} if k else {"section": 0}
+                copies.append(remote(g_out.at[g], g_back.at[g, (4 - k) % 4], b_send.at[g, k], b_recv.at[g, (4 - k) % 4], to))
+            return copies
+
         def prepare(g):
             fill_taps(0, s_shift[...], h_in[g])
             for k in (1, 3, 2):
@@ -346,17 +371,33 @@
             for t in range(TAPS):
                 acc = acc + mm(back[rows_of(8 - t)], wt[g, rows_of(t, GW), :])
             g_out[g] = acc.astype(bf)
-            copy = hop(2, g_out, g_in, g, sec - 1)
-            copy.start()
-            sends.append(copy)
+
+            @pl.when(sec == 2)
+            def hop_back():
+                hop(2, g_out, g_in, g, 1).start()
+
+            @pl.when(sec == 1)
+            def hop_to_encoders():
+                for copy in to_encoders(g):
+                    copy.start()
+
             sends += spread(gd.at[g, 0], gd, d_send, d_recv, g)
 
         @pl.when(sec == 2)
         def prepare_late():
             for g in range(2):
                 prepare(g)
-
-        for g in range(2):
+                hop(2, g_out, g_in, g, 1).wait_send()
+
+        @pl.when(sec == 1)
+        def encoders_sent():
+            for g in range(2):
+                for copy in to_encoders(g):
+                    copy.wait_send()
+
+        for g in range(2):
+            for k in (1, 3, 2):
+                spread_wait(gd.at[g, 0], gd, d_send, d_recv, g, k)
             sends += gradient(g)
         for copy in sends:
             copy.wait_send()
@@ -372,7 +413,8 @@
         turn_weights()
         for copy in loads:
             copy.wait()
-        lay_out_cells()
+        x_in[...] = jnp.zeros((CELLS, GW), bf)
+        lay_out_cells(raw)
         target[...] = mm(s_order[...], x_in[...])
         make_select()
         arrive()
@@ -477,10 +519,13 @@
             vm((4 * ROWS, GW), jnp.float32),
             vm((TAPS * ROWS, GW), bf),
             hop, hop, hop, hop, hop, hop,
-            vm((2, 4, CELLS, GW), bf),
+            vm((2, 4, 1, 12, 2, 12 * CH), bf),
             vm((2, 4, ROWS, GW), bf),
             vm((2, 4, ROWS, GW), bf),
             vm((2, 4, 4 * ROWS, GW), bf),
+            vm((2, 4, ROWS, GW), jnp.float32),
+            vm((2, 4, ROWS, GW), bf),
+            vm((2, 4, ROWS, GW), bf),
             vm((TAPS, 4 * ROWS, GW), bf),
             vm((4 * SLOT, GW), jnp.int32),
             vm((2, 2, 16 * SLOT, 4 * ROWS), bf),
@@ -490,7 +535,7 @@
             vm((4, SLOT, 2 * CH), bf),
             vm((4, SLOT, 2 * CH), bf),
             dma((10,)), dma((4, 2)), dma((4, 2)),
-            dma((2, 4)), dma((2, 4)), dma((2, 4)), dma((2, 4)), dma((2, 4)), dma((2, 4)), dma((4,)), dma((4,)),
+            *[dma((2, 4))] * 12, dma((4,)), dma((4,)),
         ],
         compiler_params=pltpu.CompilerParams(
             collective_id=0, has_side_effects=True, vmem_limit_bytes=63 * 1024 * 1024

time: 50 us -> 53.2 us (1.064)
  the two profiles are of different devices: /device:TPU:8 before, /device:TPU:1 now
where the time goes in v4:
time: 53.2 us; the launch traced here: 53.1 us
  Pallas kernels  51.6 us (97%)
  local copies, waits for them, and re-layouts  1.58 us (3%)
    pallas_call x1, Pallas kernels, on_device(): pl.pallas_call(body, out_shape=jax.ShapeDtypeStruct((SHARE, 1, 2 * CH), j...  51.6 us
    unnamed x1, local copies, waits for them, and re-layouts  1.58 us

profile of v4, /device:TPU:1, one launch (start us, length us, event | category | flops | bytes accessed | tf_op | source)
XLA Modules:
  0.0 53.1 jit_solution(10156173803375180892)
XLA Ops:
  0.0 51.6 %shard_map.73 = f32[45,1,640]{2,1,0:T(1,128)} custom-call(bf16[1,12,2,3840]{3,2,1,0:T(2,128)(2,1)} %bitcast.4, bf16[1,12,2,3840]{3,2,1,0:T(2,128)(2,1)} %bitcast.5, bf16[1,2880,640]{2,1,0:T(8,128)(2,1)} %ker.1, bf16[720,80]{1,0:T(8,128)(2,1)} %constant.8.clone.c_shift, bf16[720,384]{1,0:T(8,128)(2,1)} %constant.9.clone.c_encode, ...), custom_call_target="tpu_custom_call" | custom-call | tf_op jit(solution)/shard_map/pallas_call | solution.py:501
  51.6 1.6 %copy.9 = f32[1,45,640]{2,0,1:T(1,128)} copy(f32[1,45,640]{2,0,1:T(1,128)} %bitcast.3) | data formatting | bytes 230400

commit v5 on v3

--- a/solution.py
+++ b/solution.py
@@ -11,6 +11,7 @@
 CH = 320
 GW = 384
 TAPS = 9
+KW = TAPS * CH + 64
 SHARE = 45
 SLOT = 48
 CELLS = 12 * 32
@@ -108,7 +109,7 @@
     w_loads = []
     for n, (first, last) in enumerate(((0, GW), (GW, 2 * CH))):
         for i in range(3):
-            part = (slice(i * 960, (i + 1) * 960), slice(first, last))
+            part = (slice(i * 4 * CH, min((i + 1) * 4, TAPS) * CH), slice(first, last))
             w_loads.append(load(ker.at[(0, *part)], w_in.at[part], 4 + 3 * n + i))
     x_load = load(img, raw, 0)
     e_load = load(c_encode, s_encode, 1)
@@ -152,25 +153,38 @@
 
         def one(t, carry):
             rows = pl.ds(pl.multiple_of(t * CH, 16), CH)
-            base = pl.multiple_of(t * GW, 16)
             first = w_in[rows, 0:GW].astype(f32)
-            wp[0, pl.ds(base, CH), :] = jnp.where(lane < CH, first, 0.0).astype(bf)
+            wp[0, rows, :] = jnp.where(lane < CH, first, 0.0).astype(bf)
             second = pltpu.roll(w_in[rows, 256:640].astype(f32), GW - 64, 1)
-            wp[1, pl.ds(base, CH), :] = jnp.where(lane < CH, second, 0.0).astype(bf)
-            for g in range(2):
-                wp[g, pl.ds(base + CH, GW - CH), :] = jnp.zeros((GW - CH, GW), bf)
+            wp[1, rows, :] = jnp.where(lane < CH, second, 0.0).astype(bf)
             return carry
 
+        for g in range(2):
+            wp[g, TAPS * CH:KW, :] = jnp.zeros((64, GW), bf)
+            wt[g, TAPS * CH:KW, :] = jnp.zeros((64, GW), bf)
         lax.fori_loop(0, TAPS, one, 0)
 
     def turn_weights():
         def one(t, carry):
-            rows = pl.ds(pl.multiple_of(t * GW, 16), GW)
+            rows = pl.ds(pl.multiple_of(t * CH, 16), CH)
             for g in range(2):
-                wt[g, rows, :] = wp[g, rows, :].T
+                block = jnp.concatenate([wp[g, rows, :], jnp.zeros((GW - CH, GW), bf)], axis=0)
+                wt[g, rows, :] = block.T[0:CH]
             return carry
 
         lax.fori_loop(0, TAPS, one, 0)
+
+    def side_by_side(part, order):
+        moved = {}
+        columns = []
+        for t in range(0, TAPS - 1, 2):
+            n = order(t + 1)
+            if n not in moved:
+                moved[n] = pltpu.roll(part[rows_of(n)], 64, 1).astype(bf)
+            a, b = part[rows_of(order(t))].astype(bf), moved[n]
+            columns += [a[:, 0:256], a[:, 256:GW] + b[:, 0:128], b[:, 128:GW]]
+        columns.append(part[rows_of(order(TAPS - 1))].astype(bf))
+        return jnp.concatenate(columns, axis=1)
 
     def lay_out_cells():
         x_in[...] = jnp.zeros((CELLS, GW), bf)
@@ -250,15 +264,17 @@
         x_load.wait()
         lay_out_cells()
         e_load.wait()
-        zed[...] = mm(s_encode[...], x_in[...]).astype(bf)
+        part = mm(s_encode[...], x_in[...])
+        zed[...] = part.astype(bf)
+        feat[0, 0:ROWS, :] = side_by_side(part, lambda t: t)
         lane = lax.broadcasted_iota(jnp.int32, (ROWS, GW), 1)
         sends = []
         for g in range(2):
             acc = jnp.zeros((ROWS, GW), f32)
-            for t in range(TAPS):
-                if t % 3 == 0:
-                    w_loads[3 * g + t // 3].wait()
-                acc = acc + mm(zed[rows_of(t), 0:CH], w_in[rows_of(t, CH), g * 256:g * 256 + GW])
+            for i in range(3):
+                w_loads[3 * g + i].wait()
+                rows = slice(i * 4 * CH, min((i + 1) * 4, TAPS) * CH)
+                acc = acc + mm(feat[0, 0:ROWS, rows], w_in[rows, g * 256:g * 256 + GW])
             if g:
                 acc = pltpu.roll(acc, GW - 64, 1)
             acc = jnp.where(lane < CH, acc, 0.0)
@@ -307,10 +323,7 @@
         sends = []
         for g in range(2):
             hop(0, h_out, h_in, g, sec - 1).wait_recv()
-            shifted = mm(s_shift[...], h_in[g]).astype(bf)
-            acc = jnp.zeros((ROWS, GW), f32)
-            for t in range(TAPS):
-                acc = acc + mm(shifted[rows_of(t)], wp[g, rows_of(t, GW), :])
+            acc = mm(side_by_side(mm(s_shift[...], h_in[g]), lambda t: t), wp[g])
             act[g] = acc
             h_out[g] = (h_in[g].astype(f32) + silu(acc)).astype(bf)
             copy = hop(0, h_out, h_in, g, sec + 1)
@@ -341,11 +354,8 @@
             hop(2, g_out, g_in, g, sec + 1).wait_recv()
             delta = (g_in[g].astype(f32) * silu_slope(act[g])).astype(bf)
             gd[g, 0] = delta
-            back = mm(s_shift[...], delta).astype(bf)
-            acc = g_in[g].astype(f32)
-            for t in range(TAPS):
-                acc = acc + mm(back[rows_of(8 - t)], wt[g, rows_of(t, GW), :])
-            g_out[g] = acc.astype(bf)
+            back = mm(side_by_side(mm(s_shift[...], delta), lambda t: 8 - t), wt[g])
+            g_out[g] = (g_in[g].astype(f32) + back).astype(bf)
             copy = hop(2, g_out, g_in, g, sec - 1)
             copy.start()
             sends.append(copy)
@@ -383,10 +393,9 @@
             u = (h_in[g].astype(f32) + skip_in[g].astype(f32)).astype(bf)
             gh[g, 0] = u
             sends += spread(gh.at[g, 0], gh, a_send, a_recv, g)
-            shifted = mm(s_shift[...], u).astype(bf)
+            shifted = mm(s_shift[...], u)
             for phase in range(4):
-                for t in range(TAPS):
-                    feat[g, rows_of(phase), rows_of(t, GW)] = shifted[rows_of(phase_shift(phase, t))]
+                feat[g, rows_of(phase), :] = side_by_side(shifted, lambda t: phase_shift(phase, t))
             pre[g] = mm(feat[g], wp[g])
         value, gate = pre[0], pre[1]
         sig = jax.nn.sigmoid(gate)
@@ -397,11 +406,7 @@
         for g in range(2):
             sends += spread(gd3.at[g, 0], gd3, d_send, d_recv, g)
         for g in range(2):
-            back = mm(s_fold[...], gd3[g, 0]).astype(bf)
-            acc = jnp.zeros((ROWS, GW), f32)
-            for t in range(TAPS):
-                acc = acc + mm(back[rows_of(t)], wt[g, rows_of(t, GW), :])
-            g_out[g] = acc.astype(bf)
+            g_out[g] = mm(side_by_side(mm(s_fold[...], gd3[g, 0]), lambda t: t), wt[g]).astype(bf)
             for copy in (hop(2, g_out, g_in, g, 2), hop(3, g_out, gskip_in, g, 0)):
                 copy.start()
                 sends.append(copy)
@@ -469,9 +474,9 @@
             vm((TAPS * ROWS, CELLS), bf),
             vm((TAPS * ROWS, 4 * ROWS), bf),
             vm((4 * ROWS, CELLS), bf),
-            vm((2, TAPS * GW, GW), bf),
-            vm((2, TAPS * GW, GW), bf),
-            vm((2, 4 * ROWS, TAPS * GW), bf),
+            vm((2, KW, GW), bf),
+            vm((2, KW, GW), bf),
+            vm((2, 4 * ROWS, KW), bf),
             vm((2, ROWS, GW), jnp.float32),
             vm((2, 4 * ROWS, GW), jnp.float32),
             vm((4 * ROWS, GW), jnp.float32),

time: 50 us -> 48.1 us (0.962)
  Pallas kernels: 48.3 us -> 46.3 us
    pallas_call x1, Pallas kernels: 48.3 us -> 46.3 us  [on_device(): pl.pallas_call(body, out_shape=jax.ShapeDtypeStruct((SHARE, 1, 2 * CH), j...]
where the time goes in v5:
time: 48.1 us; the launch traced here: 47.8 us
  Pallas kernels  46.3 us (96%)
  local copies, waits for them, and re-layouts  1.58 us (3%)
    pallas_call x1, Pallas kernels, on_device(): pl.pallas_call(body, out_shape=jax.ShapeDtypeStruct((SHARE, 1, 2 * CH), j...  46.3 us
    unnamed x1, local copies, waits for them, and re-layouts  1.58 us

profile of v5, /device:TPU:8, one launch (start us, length us, event | category | flops | bytes accessed | tf_op | source)
XLA Modules:
  0.0 47.8 jit_solution(16966098076936582054)
XLA Ops:
  0.0 46.3 %shard_map.73 = f32[45,1,640]{2,1,0:T(1,128)} custom-call(bf16[1,12,2,3840]{3,2,1,0:T(2,128)(2,1)} %bitcast.4, bf16[1,12,2,3840]{3,2,1,0:T(2,128)(2,1)} %bitcast.5, bf16[1,2880,640]{2,1,0:T(8,128)(2,1)} %ker.1, bf16[720,80]{1,0:T(8,128)(2,1)} %constant.8.clone.c_shift, bf16[720,384]{1,0:T(8,128)(2,1)} %constant.9.clone.c_encode, ...), custom_call_target="tpu_custom_call" | custom-call | tf_op jit(solution)/shard_map/pallas_call | solution.py:464
  46.3 1.6 %copy.9 = f32[1,45,640]{2,0,1:T(1,128)} copy(f32[1,45,640]{2,0,1:T(1,128)} %bitcast.3) | data formatting | bytes 230400

commit v6 on v5

--- a/solution.py
+++ b/solution.py
@@ -133,7 +133,7 @@
 
     def spread(src, buf, send, recv, g):
         copies = []
-        for k in (1, 3, 2):
+        for k in (2, 1, 3):
             copy = remote(src, buf.at[g, 4 - k], send.at[g, k], recv.at[g, 4 - k], gather_peer[g](k))
             copy.start()
             copies.append(copy)
@@ -359,6 +359,7 @@
             copy = hop(2, g_out, g_in, g, sec - 1)
             copy.start()
             sends.append(copy)
+        for g in range(2):
             sends += spread(gd.at[g, 0], gd, d_send, d_recv, g)
 
         @pl.when(sec == 2)
@@ -392,11 +393,11 @@
             hop(0, h_out, h_in, g, 2).wait_recv()
             u = (h_in[g].astype(f32) + skip_in[g].astype(f32)).astype(bf)
             gh[g, 0] = u
-            sends += spread(gh.at[g, 0], gh, a_send, a_recv, g)
             shifted = mm(s_shift[...], u)
             for phase in range(4):
                 feat[g, rows_of(phase), :] = side_by_side(shifted, lambda t: phase_shift(phase, t))
             pre[g] = mm(feat[g], wp[g])
+            sends += spread(gh.at[g, 0], gh, a_send, a_recv, g)
         value, gate = pre[0], pre[1]
         sig = jax.nn.sigmoid(gate)
         act_gate = gate * sig
@@ -404,12 +405,11 @@
         gd3[0, 0] = (residual * act_gate).astype(bf)
         gd3[1, 0] = (residual * value * (sig * (1.0 + gate * (1.0 - sig)))).astype(bf)
         for g in range(2):
-            sends += spread(gd3.at[g, 0], gd3, d_send, d_recv, g)
-        for g in range(2):
             g_out[g] = mm(side_by_side(mm(s_fold[...], gd3[g, 0]), lambda t: t), wt[g]).astype(bf)
             for copy in (hop(2, g_out, g_in, g, 2), hop(3, g_out, gskip_in, g, 0)):
                 copy.start()
                 sends.append(copy)
+            sends += spread(gd3.at[g, 0], gd3, d_send, d_recv, g)
         for g in range(2):
             for k in (1, 3, 2):
                 spread_wait(gh.at[g, 0], gh, a_send, a_recv, g, k)

time: 48.1 us -> 50.1 us (1.042)
  the two profiles are of different devices: /device:TPU:8 before, /device:TPU:1 now
where the time goes in v6:
time: 50.1 us; the launch traced here: 50 us
  Pallas kernels  48.4 us (97%)
  local copies, waits for them, and re-layouts  1.58 us (3%)
    pallas_call x1, Pallas kernels, on_device(): pl.pallas_call(body, out_shape=jax.ShapeDtypeStruct((SHARE, 1, 2 * CH), j...  48.4 us
    unnamed x1, local copies, waits for them, and re-layouts  1.58 us

profile of v6, /device:TPU:1, one launch (start us, length us, event | category | flops | bytes accessed | tf_op | source)
XLA Modules:
  0.0 50.0 jit_solution(15572332838867300277)
XLA Ops:
  0.0 48.4 %shard_map.73 = f32[45,1,640]{2,1,0:T(1,128)} custom-call(bf16[1,12,2,3840]{3,2,1,0:T(2,128)(2,1)} %bitcast.4, bf16[1,12,2,3840]{3,2,1,0:T(2,128)(2,1)} %bitcast.5, bf16[1,2880,640]{2,1,0:T(8,128)(2,1)} %ker.1, bf16[720,80]{1,0:T(8,128)(2,1)} %constant.8.clone.c_shift, bf16[720,384]{1,0:T(8,128)(2,1)} %constant.9.clone.c_encode, ...), custom_call_target="tpu_custom_call" | custom-call | tf_op jit(solution)/shard_map/pallas_call | solution.py:464
  48.4 1.6 %copy.9 = f32[1,45,640]{2,0,1:T(1,128)} copy(f32[1,45,640]{2,0,1:T(1,128)} %bitcast.3) | data formatting | bytes 230400

commit v7 on v6

--- a/solution.py
+++ b/solution.py
@@ -133,7 +133,7 @@
 
     def spread(src, buf, send, recv, g):
         copies = []
-        for k in (2, 1, 3):
+        for k in (1, 3, 2):
             copy = remote(src, buf.at[g, 4 - k], send.at[g, k], recv.at[g, 4 - k], gather_peer[g](k))
             copy.start()
             copies.append(copy)
@@ -354,13 +354,12 @@
             hop(2, g_out, g_in, g, sec + 1).wait_recv()
             delta = (g_in[g].astype(f32) * silu_slope(act[g])).astype(bf)
             gd[g, 0] = delta
+            sends += spread(gd.at[g, 0], gd, d_send, d_recv, g)
             back = mm(side_by_side(mm(s_shift[...], delta), lambda t: 8 - t), wt[g])
             g_out[g] = (g_in[g].astype(f32) + back).astype(bf)
             copy = hop(2, g_out, g_in, g, sec - 1)
             copy.start()
             sends.append(copy)
-        for g in range(2):
-            sends += spread(gd.at[g, 0], gd, d_send, d_recv, g)
 
         @pl.when(sec == 2)
         def prepare_late():

time: 50.1 us -> 47.3 us (0.944)
  the two profiles are of different devices: /device:TPU:1 before, /device:TPU:8 now
where the time goes in v7:
time: 47.3 us; the launch traced here: 47.2 us
  Pallas kernels  45.6 us (96%)
  local copies, waits for them, and re-layouts  1.58 us (3%)
    pallas_call x1, Pallas kernels, on_device(): pl.pallas_call(body, out_shape=jax.ShapeDtypeStruct((SHARE, 1, 2 * CH), j...  45.6 us
    unnamed x1, local copies, waits for them, and re-layouts  1.58 us

profile of v7, /device:TPU:8, one launch (start us, length us, event | category | flops | bytes accessed | tf_op | source)
XLA Modules:
  0.0 47.2 jit_solution(6060093643277741311)
XLA Ops:
  0.0 45.6 %shard_map.73 = f32[45,1,640]{2,1,0:T(1,128)} custom-call(bf16[1,12,2,3840]{3,2,1,0:T(2,128)(2,1)} %bitcast.4, bf16[1,12,2,3840]{3,2,1,0:T(2,128)(2,1)} %bitcast.5, bf16[1,2880,640]{2,1,0:T(8,128)(2,1)} %ker.1, bf16[720,80]{1,0:T(8,128)(2,1)} %constant.8.clone.c_shift, bf16[720,384]{1,0:T(8,128)(2,1)} %constant.9.clone.c_encode, ...), custom_call_target="tpu_custom_call" | custom-call | tf_op jit(solution)/shard_map/pallas_call | solution.py:463
  45.6 1.6 %copy.9 = f32[1,45,640]{2,0,1:T(1,128)} copy(f32[1,45,640]{2,0,1:T(1,128)} %bitcast.3) | data formatting | bytes 230400

commit v8 on v7

--- a/solution.py
+++ b/solution.py
@@ -133,7 +133,7 @@
 
     def spread(src, buf, send, recv, g):
         copies = []
-        for k in (1, 3, 2):
+        for k in (2, 1, 3):
             copy = remote(src, buf.at[g, 4 - k], send.at[g, k], recv.at[g, 4 - k], gather_peer[g](k))
             copy.start()
             copies.append(copy)

time: 47.3 us -> 47.5 us (level); the launches traced: 47.2 us -> 46.8 us
  no operation moved by 1% of the time
where the time goes in v8:
time: 47.5 us; the launch traced here: 46.8 us
  Pallas kernels  45.2 us (95%)
  local copies, waits for them, and re-layouts  1.58 us (3%)
    pallas_call x1, Pallas kernels, on_device(): pl.pallas_call(body, out_shape=jax.ShapeDtypeStruct((SHARE, 1, 2 * CH), j...  45.2 us
    unnamed x1, local copies, waits for them, and re-layouts  1.58 us

profile of v8, /device:TPU:8, one launch (start us, length us, event | category | flops | bytes accessed | tf_op | source)
XLA Modules:
  0.0 46.8 jit_solution(12540024947625317455)
XLA Ops:
  0.0 45.2 %shard_map.73 = f32[45,1,640]{2,1,0:T(1,128)} custom-call(bf16[1,12,2,3840]{3,2,1,0:T(2,128)(2,1)} %bitcast.4, bf16[1,12,2,3840]{3,2,1,0:T(2,128)(2,1)} %bitcast.5, bf16[1,2880,640]{2,1,0:T(8,128)(2,1)} %ker.1, bf16[720,80]{1,0:T(8,128)(2,1)} %constant.8.clone.c_shift, bf16[720,384]{1,0:T(8,128)(2,1)} %constant.9.clone.c_encode, ...), custom_call_target="tpu_custom_call" | custom-call | tf_op jit(solution)/shard_map/pallas_call | solution.py:463
  45.2 1.6 %copy.9 = f32[1,45,640]{2,0,1:T(1,128)} copy(f32[1,45,640]{2,0,1:T(1,128)} %bitcast.3) | data formatting | bytes 230400

commit v9 on v7

--- a/solution.py
+++ b/solution.py
@@ -186,13 +186,12 @@
         columns.append(part[rows_of(order(TAPS - 1))].astype(bf))
         return jnp.concatenate(columns, axis=1)
 
-    def lay_out_cells():
-        x_in[...] = jnp.zeros((CELLS, GW), bf)
+    def lay_out_cells(grids):
         lane = lax.broadcasted_iota(jnp.int32, (12, GW), 1)
         for n in range(2):
             for j in range(12):
                 start = j * CH - 64 * (j % 2)
-                part = raw[0, :, n, start:start + GW].astype(f32)
+                part = grids[0, :, n, start:start + GW].astype(f32)
                 if j % 2:
                     part = pltpu.roll(part, GW - 64, 1)
                 x_in[j * 32 + n * 16:j * 32 + n * 16 + 12, :] = jnp.where(lane < CH, part, 0.0).astype(bf)
@@ -261,8 +260,9 @@
 
     @pl.when(sec == 0)
     def encoder():
+        x_in[...] = jnp.zeros((CELLS, GW), bf)
         x_load.wait()
-        lay_out_cells()
+        lay_out_cells(raw)
         e_load.wait()
         part = mm(s_encode[...], x_in[...])
         zed[...] = part.astype(bf)
@@ -286,14 +286,15 @@
                 copy.start()
                 sends.append(copy)
         for g in range(2):
-            sends += spread(x_in, gx, a_send, a_recv, g)
+            sends += spread(raw, gx, a_send, a_recv, g)
         make_select()
         for g in range(2):
             for t in range(TAPS):
                 taps[t, rows_of(0), :] = zed[rows_of(t)]
             for k in (1, 3, 2):
-                spread_wait(x_in, gx, a_send, a_recv, g, k)
-                fill_taps(k, s_encode[...], gx[g, k])
+                spread_wait(raw, gx, a_send, a_recv, g, k)
+                lay_out_cells(gx.at[g, k])
+                fill_taps(k, s_encode[...], x_in[...])
             make_left(g)
         for g in range(2):
             hop(3, g_out, gskip_in, g, 3).wait_recv()
@@ -382,7 +383,8 @@
         turn_weights()
         for copy in loads:
             copy.wait()
-        lay_out_cells()
+        x_in[...] = jnp.zeros((CELLS, GW), bf)
+        lay_out_cells(raw)
         target[...] = mm(s_order[...], x_in[...])
         make_select()
         arrive()
@@ -481,7 +483,7 @@
             vm((4 * ROWS, GW), jnp.float32),
             vm((TAPS * ROWS, GW), bf),
             hop, hop, hop, hop, hop, hop,
-            vm((2, 4, CELLS, GW), bf),
+            vm((2, 4, 1, 12, 2, 12 * CH), bf),
             vm((2, 4, ROWS, GW), bf),
             vm((2, 4, ROWS, GW), bf),
             vm((2, 4, 4 * ROWS, GW), bf),

time: 47.3 us -> 47.1 us (level)
  no operation moved by 1% of the time
where the time goes in v9:
time: 47.1 us; the launch traced here: 47 us
  Pallas kernels  45.4 us (96%)
  local copies, waits for them, and re-layouts  1.58 us (3%)
    pallas_call x1, Pallas kernels, on_device(): pl.pallas_call(body, out_shape=jax.ShapeDtypeStruct((SHARE, 1, 2 * CH), j...  45.4 us
    unnamed x1, local copies, waits for them, and re-layouts  1.58 us

profile of v9, /device:TPU:8, one launch (start us, length us, event | category | flops | bytes accessed | tf_op | source)
XLA Modules:
  0.0 47.0 jit_solution(17059572415231801507)
XLA Ops:
  0.0 45.4 %shard_map.73 = f32[45,1,640]{2,1,0:T(1,128)} custom-call(bf16[1,12,2,3840]{3,2,1,0:T(2,128)(2,1)} %bitcast.4, bf16[1,12,2,3840]{3,2,1,0:T(2,128)(2,1)} %bitcast.5, bf16[1,2880,640]{2,1,0:T(8,128)(2,1)} %ker.1, bf16[720,80]{1,0:T(8,128)(2,1)} %constant.8.clone.c_shift, bf16[720,384]{1,0:T(8,128)(2,1)} %constant.9.clone.c_encode, ...), custom_call_target="tpu_custom_call" | custom-call | tf_op jit(solution)/shard_map/pallas_call | solution.py:465
  45.4 1.6 %copy.9 = f32[1,45,640]{2,0,1:T(1,128)} copy(f32[1,45,640]{2,0,1:T(1,128)} %bitcast.3) | data formatting | bytes 230400
